TPU v7x, 128 devices: a whole 4x4x4 slice. The times are simulated.
128 devices in a mesh: img: 64 (over z, y, x), mdl: 2 (over core).
Axes of the slice: x: 4, y: 4, z: 4, core: 2. Of those that a mesh axis runs over, the one named last changes fastest.
Arguments:
- tokens: bfloat16 [512, 196, 1024], P('img', None, 'mdl'), may hold values from -16 to 16
- image_row: int32 [512], replicated, may hold values from 0 to 511, as said below
- views: int32 [64, 16], replicated, may hold values from 0 to 511, as said below
- pairs: int32 [64, 8, 2], P('img'), may hold values from 0 to 15, as said below
- pair_count: int32 [64], P('img'), may hold values from 4 to 8, as said below
- w_query: bfloat16 [1024, 1024], P(None, 'mdl'), may hold values from -0.1875 to 0.1875
- w_key: bfloat16 [1024, 1024], P(None, 'mdl'), may hold values from -0.1875 to 0.1875
- w_value: bfloat16 [1024, 1024], P(None, 'mdl'), may hold values from -0.1875 to 0.1875
- w_out: bfloat16 [1024, 1024], P('mdl'), may hold values from -0.1875 to 0.1875
- head_in: bfloat16 [1024, 256], P('mdl'), may hold values from -0.1875 to 0.1875
- head_mid: bfloat16 [256, 256], replicated, may hold values from -0.375 to 0.375
- head_last: bfloat16 [4, 256], replicated, may hold values from -0.375 to 0.375
Outputs:
- joined: float32 [512, 3, 196], P('img')
- weight_total: float32 [512, 196], P('img')
Inputs may be any that keep to these rules, and one draw needn't show every extreme that they name: `image_row`: a permutation of the 512 storage rows. `views`: each row holds 16 distinct image ids; at most 1 of one row's images are stored on one index of img, and some index of img stores exactly 1 of them. `pairs`: the two entries of a pair differ. `pair_count`: the live pairs are the leading ones; some pair device has 8.
All inputs are finite; a program needn't handle non-finite values.
Results may differ from a plain program's by a relative error of at most 0.025.
Values may be sent and summed in bfloat16 or wider, within the bound.
No kernel may reach another device: no remote copies, remote signals or barrier semaphores. Data moves between devices by JAX's collectives and lax.ppermute only.
A program may use at most 128 MiB of HBM per device.

v0:
```python
import jax
import jax.numpy as jnp
from jax import lax
from jax.sharding import PartitionSpec as P

D = 1024
HEAD_DIM = 64


def local(
    tokens,
    image_row,
    views,
    pairs,
    pair_count,
    w_query,
    w_key,
    w_value,
    w_out,
    head_in,
    head_mid,
    head_last,
):
    groups = lax.axis_size("img")
    own_index = lax.axis_index("img")
    parts_mdl = lax.axis_size("mdl")
    part_index = lax.axis_index("mdl")
    img_dev, tokens_per, quarter = tokens.shape
    view_cap = views.shape[1]
    link_cap = (view_cap + groups - 1) // groups
    stored = image_row[views]
    owners = stored // img_dev
    local_slot = stored % img_dev
    view_order = jnp.arange(view_cap)
    earlier = (owners[:, :, None] == owners[:, None, :]) & (
        view_order[None, None, :] < view_order[None, :, None]
    )
    link_pos = jnp.sum(earlier.astype(jnp.int32), axis=2)
    is_mine = owners == own_index
    slot_hits = (
        is_mine[:, :, None, None]
        & (link_pos[:, :, None, None] == jnp.arange(link_cap)[None, None, :, None])
        & (local_slot[:, :, None, None] == jnp.arange(img_dev)[None, None, None, :])
    )
    select = jnp.any(slot_hits, axis=1).astype(jnp.bfloat16)
    outgoing = jnp.einsum(
        "ntl,lrf->ntrf", select, tokens, preferred_element_type=jnp.float32
    ).astype(jnp.bfloat16)
    arriving = lax.all_to_all(outgoing, "img", split_axis=0, concat_axis=0, tiled=True)
    my_owner = lax.dynamic_index_in_dim(owners, own_index, 0, keepdims=False)
    my_link = lax.dynamic_index_in_dim(link_pos, own_index, 0, keepdims=False)
    view_rows = jnp.take(
        arriving.reshape(groups * link_cap, tokens_per, quarter),
        my_owner * link_cap + my_link,
        axis=0,
    )
    head_cols = w_query.shape[1]
    shard_piece = lax.all_gather(view_rows, "mdl", axis=2, tiled=True)
    queries = jnp.einsum(
        "vtf,fc->vtc", shard_piece, w_query, preferred_element_type=jnp.float32
    ).astype(jnp.bfloat16)
    keys_local = jnp.einsum(
        "vtf,fc->vtc", shard_piece, w_key, preferred_element_type=jnp.float32
    ).astype(jnp.bfloat16)
    values_local = jnp.einsum(
        "vtf,fc->vtc", shard_piece, w_value, preferred_element_type=jnp.float32
    ).astype(jnp.bfloat16)
    slot_pairs = pairs[0]
    pair_slots = slot_pairs.shape[0]
    query_view = slot_pairs.reshape(2 * pair_slots)
    key_view = slot_pairs[:, ::-1].reshape(2 * pair_slots)
    slot_total = 2 * pair_slots
    head_count = head_cols // HEAD_DIM
    query_heads = jnp.take(queries, query_view, axis=0).reshape(
        slot_total, tokens_per, head_count, HEAD_DIM
    )
    key_heads = jnp.take(keys_local, key_view, axis=0).reshape(
        slot_total, tokens_per, head_count, HEAD_DIM
    )
    value_heads = jnp.take(values_local, key_view, axis=0).reshape(
        slot_total, tokens_per, head_count, HEAD_DIM
    )
    scores = jnp.einsum(
        "sqhd,skhd->shqk", query_heads, key_heads, preferred_element_type=jnp.float32
    ) * HEAD_DIM ** (-0.5)
    weights = jnp.exp(scores)
    probs = (weights / jnp.sum(weights, axis=-1, keepdims=True)).astype(jnp.bfloat16)
    attended = jnp.einsum("shqk,skhd->sqhd", probs, value_heads, preferred_element_type=jnp.float32)
    attended = attended.astype(jnp.bfloat16).reshape(slot_total, tokens_per, head_cols)
    own_rows = jnp.take(view_rows, query_view, axis=0)
    share = slot_total // parts_mdl
    first_slot = part_index * share
    partial_out = jnp.einsum("stc,cd->std", attended, w_out, preferred_element_type=jnp.float32)
    mixed = own_rows.astype(jnp.float32) + lax.psum_scatter(
        partial_out.astype(jnp.bfloat16), "mdl", scatter_dimension=2, tiled=True
    ).astype(jnp.float32)
    feature_sum, square_sum = lax.psum(
        (jnp.sum(mixed, axis=-1), jnp.sum(mixed * mixed, axis=-1)), "mdl"
    )
    mean_row = feature_sum / D
    scale_row = lax.rsqrt(square_sum / D - mean_row * mean_row + 1e-05)
    normed = ((mixed - mean_row[..., None]) * scale_row[..., None]).astype(jnp.bfloat16)
    first_layer = lax.psum(
        jnp.einsum("stf,fh->sth", normed, head_in, preferred_element_type=jnp.float32).astype(
            jnp.bfloat16
        ),
        "mdl",
    ).astype(jnp.float32)
    first_layer = lax.dynamic_slice_in_dim(first_layer, first_slot, share, 0)
    hidden = jax.nn.gelu(first_layer).astype(jnp.bfloat16)
    inner = jax.nn.gelu(
        jnp.einsum("sth,hk->stk", hidden, head_mid, preferred_element_type=jnp.float32)
    ).astype(jnp.bfloat16)
    head_out = jnp.einsum("stk,ck->sct", inner, head_last, preferred_element_type=jnp.float32)
    slot_live = (jnp.repeat(jnp.arange(pair_slots), 2) < pair_count[0]).astype(jnp.float32)
    share_live = lax.dynamic_slice_in_dim(slot_live, first_slot, share, 0)
    share_query = lax.dynamic_slice_in_dim(query_view, first_slot, share, 0)
    confidence = (1.0 + jax.nn.softplus(head_out[:, 3, :])) * share_live[:, None]
    weighted = head_out[:, :3, :] * confidence[:, None, :]
    destination = my_owner[share_query] * link_cap + my_link[share_query]
    placing = (destination[None, :] == jnp.arange(groups * link_cap)[:, None]).astype(jnp.float32)
    send_points = jnp.einsum(
        "gs,sct->gct", placing, weighted, precision=lax.Precision.HIGHEST
    ).reshape(groups, link_cap, 3, tokens_per)
    send_conf = jnp.einsum(
        "gs,st->gt", placing, confidence, precision=lax.Precision.HIGHEST
    ).reshape(groups, link_cap, tokens_per)
    select_float = select.astype(jnp.float32)
    summed_points, summed_conf = (
        lax.psum(send_points.astype(jnp.bfloat16), "mdl").astype(jnp.float32),
        lax.psum(send_conf.astype(jnp.bfloat16), "mdl").astype(jnp.float32),
    )
    back_points, back_conf = (
        lax.all_to_all(
            summed_points.astype(jnp.bfloat16), "img", split_axis=0, concat_axis=0, tiled=True
        ).astype(summed_points.dtype),
        lax.all_to_all(
            summed_conf.astype(jnp.bfloat16), "img", split_axis=0, concat_axis=0, tiled=True
        ).astype(summed_conf.dtype),
    )
    numerator = jnp.einsum(
        "ntl,ntcr->lcr", select_float, back_points, precision=lax.Precision.HIGHEST
    )
    weight_total = jnp.einsum(
        "ntl,ntr->lr", select_float, back_conf, precision=lax.Precision.HIGHEST
    )
    joined = numerator / jnp.maximum(weight_total, 1.0)[:, None, :]
    return (joined, weight_total)


def solution(mesh):
    placed = (
        P("img", None, "mdl"),
        P(),
        P(),
        P("img", None, None),
        P("img"),
        P(None, "mdl"),
        P(None, "mdl"),
        P(None, "mdl"),
        P("mdl", None),
        P("mdl", None),
        P(),
        P(),
    )
    return jax.shard_map(
        local,
        mesh=mesh,
        in_specs=placed,
        out_specs=(P("img", None, None), P("img", None)),
        check_vma=False,
    )
```

profile of v0, /device:TPU:1, one launch (start us, length us, event | category | flops | bytes accessed | tf_op | source)
XLA Modules:
  0.0 505.6 jit_solution(15914460666152028304)
XLA Ops:
  7.2 0.8 compare_select_fusion.2
  8.0 0.1 copy.73
  8.1 0.1 reshape.246
  8.2 6.9 %gather_fusion = s32[1024]{0:T(1024)S(1)} fusion(s32[512]{0:T(512)S(1)} %copy-done.2, s32[1024]{0:T(1024)S(1)} %broadcast_clamp_fusion), kind=kCustom, calls=%fused_computation.4 | custom fusion | bytes 12288 | tf_op jit(solution)/shard_map/gather | solution.py:31
  15.1 0.1 reshape.245
  15.2 0.1 copy.74
  15.3 0.1 convert_reduce_fusion
  15.4 6.6 %convert_bitcast_fusion = bf16[64,1,196,512]{3,0,2,1:T(8,128)(2,1)} fusion(bf16[8,196,512]{2,0,1:T(8,128)(2,1)S(1)} %copy-done, pred[64,8]{0,1:T(8,128)(4,1)S(1)} %fusion.48), kind=kOutput, calls=%fused_computation.12 | convolution fusion | flops 109182976 | bytes 14451200 | tf_op jit(solution)/shard_map/ntl,lrf->ntrf/dot_general | solution.py:46
  22.0 11.2 %copy.79 = bf16[64,1,196,512]{3,2,1,0:T(8,128)(2,1)} copy(bf16[64,1,196,512]{3,0,2,1:T(8,128)(2,1)} %convert_bitcast_fusion) | data formatting | bytes 25690112 | tf_op jit(solution)/shard_map/convert_element_type | solution.py:48
  33.2 12.2 %all-to-all-start = ((bf16[64,1,196,512]{3,2,1,0:T(8,128)(2,1)}), bf16[64,1,196,512]{3,2,1,0:T(8,128)(2,1)}, u32[]{:S(2)}, u32[]{:S(2)}) async-start(bf16[64,1,196,512]{3,2,1,0:T(8,128)(2,1)} %copy.79), calls=%async_computation | async-start | bytes 26214400 | tf_op jit(solution)/shard_map/all_to_all | solution.py:49
  45.4 0.0 all-gather.2.cloned.1.call-start
  45.5 0.2 dynamic-slice_reduce_fusion
  45.7 206.0 %all-to-all-done = bf16[64,1,196,512]{3,2,1,0:T(8,128)(2,1)} async-done(((bf16[64,1,196,512]{3,2,1,0:T(8,128)(2,1)}), bf16[64,1,196,512]{3,2,1,0:T(8,128)(2,1)}, u32[]{:S(2)}, u32[]{:S(2)}) %all-to-all-start) | async-done | bytes 12845088 | tf_op jit(solution)/shard_map/all_to_all | solution.py:49
  251.8 7.2 %gather_fusion.3 = bf16[16,196,512]{2,1,0:T(8,128)(2,1)} fusion(bf16[64,196,512]{2,1,0:T(8,128)(2,1)} %bitcast.3, s32[1024]{0:T(1024)S(1)} %pad_clamp_fusion.2), kind=kCustom, calls=%fused_computation.7 | custom fusion | bytes 6422592 | tf_op jit(solution)/shard_map/jit(_take)/gather | solution.py:52
  258.9 4.0 broadcast_select_fusion.4
  262.9 0.0 all-gather.2.cloned.1.call-update
  263.0 0.2 reduce-scatter.2.cloned.1.call-start
  263.2 0.4 copy-done.3
  263.6 0.1 copy.78
  263.7 0.1 copy.80
  263.8 0.1 reshape.204
  263.9 0.1 reshape_squeeze.3
  264.0 20.5 %all-gather.2.cloned.1.call-done = bf16[16,196,1024]{2,1,0:T(8,128)(2,1)} async-done(((bf16[16,196,512]{2,1,0:T(8,128)(2,1)}), bf16[16,196,1024]{2,1,0:T(8,128)(2,1)}) %all-gather.2.cloned.1.call-update) | async-done | bytes 6422544 | tf_op jit(solution)/shard_map/all_gather | solution.py:58
  284.5 7.9 %convolution_convert_fusion.1 = bf16[16,196,512]{2,1,0:T(8,128)(2,1)} fusion(bf16[16,196,1024]{2,1,0:T(8,128)(2,1)} %all-gather.2.cloned.1.call-done, bf16[1024,512]{1,0:T(8,128)(2,1)S(1)} %copy-done.4), kind=kOutput, calls=%fused_computation.32 | convolution fusion | flops 3289939968 | bytes 10682368 | tf_op jit(solution)/shard_map/vtf,fc->vtc/dot_general | solution.py:62
  292.4 4.5 gather_fusion.7
  296.9 7.8 %convolution_convert_fusion.3 = bf16[16,196,512]{2,1,0:T(8,128)(2,1)} fusion(bf16[16,196,1024]{2,1,0:T(8,128)(2,1)} %all-gather.2.cloned.1.call-done, bf16[1024,512]{1,0:T(8,128)(2,1)S(1)} %copy-done.5), kind=kOutput, calls=%fused_computation.34 | convolution fusion | flops 3289939968 | bytes 10682368 | tf_op jit(solution)/shard_map/vtf,fc->vtc/dot_general | solution.py:65
  304.7 4.4 gather_fusion.5
  309.1 6.3 %broadcast_select_fusion = (bf16[16,196,512]{2,1,0:T(8,128)(2,1)}, bf16[16,196,512]{2,1,0:T(8,128)(2,1)}) fusion(bf16[16,196,512]{2,1,0:T(8,128)(2,1)} %gather_fusion.7, pred[16]{0:T(512)(128)(4,1)S(1)} %get-tuple-element.22, bf16[16,196,512]{2,1,0:T(8,128)(2,1)} %gather_fusion.5), kind=kLoop, calls=%fused_computation.21 | loop fusion | flops 3211264 | bytes 12845072 | tf_op jit(solution)/shard_map/jit(_take)/select_n | solution.py:77
  315.4 6.1 %copy.83 = bf16[16,196,512]{1,2,0:T(8,128)(2,1)} copy(bf16[16,196,512]{2,1,0:T(8,128)(2,1)} %get-tuple-element.16) | data formatting | bytes 6422528 | tf_op jit(solution)/shard_map/jit(_take)/select_n | solution.py:77
  321.5 7.9 %convolution_convert_fusion.2 = bf16[16,196,512]{2,1,0:T(8,128)(2,1)} fusion(bf16[16,196,1024]{2,1,0:T(8,128)(2,1)} %all-gather.2.cloned.1.call-done, bf16[1024,512]{1,0:T(8,128)(2,1)S(1)} %copy-done.6), kind=kOutput, calls=%fused_computation.33 | convolution fusion | flops 3289939968 | bytes 10682368 | tf_op jit(solution)/shard_map/vtf,fc->vtc/dot_general | solution.py:59
  329.4 4.3 gather_fusion.6
  333.7 3.9 broadcast_select_fusion.2
  337.7 6.0 %copy.82 = bf16[16,196,512]{1,2,0:T(8,128)(2,1)} copy(bf16[16,196,512]{2,1,0:T(8,128)(2,1)} %broadcast_select_fusion.2) | data formatting | bytes 6422528 | tf_op jit(solution)/shard_map/jit(_take)/select_n | solution.py:74
  343.7 6.0 %copy.81 = bf16[16,196,512]{1,2,0:T(8,128)(2,1)} copy(bf16[16,196,512]{2,1,0:T(8,128)(2,1)} %get-tuple-element.17) | data formatting | bytes 6422528 | tf_op jit(solution)/shard_map/jit(_take)/select_n | solution.py:80
  349.7 17.3 %fusion = (f32[16,8,196]{2,1,0:T(8,128)S(1)}, f32[16,8,196,196]{2,3,1,0:T(8,128)}) fusion(bf16[16,196,8,64]{1,3,2,0:T(8,128)(2,1)} %bitcast.94, bf16[16,196,8,64]{1,3,2,0:T(8,128)(2,1)} %bitcast.93), kind=kOutput, calls=%fused_computation.10 | convolution fusion | flops 639217152 | bytes 26191872 | tf_op jit(solution)/shard_map/sqhd,skhd->shqk/dot_general | solution.py:83
  367.0 14.3 %fusion.6 = bf16[16,8,64,196]{3,2,1,0:T(8,128)(2,1)} fusion(bf16[16,196,8,64]{1,3,2,0:T(8,128)(2,1)} %bitcast.95, f32[16,8,196,196]{2,3,1,0:T(8,128)} %get-tuple-element.19, f32[16,8,196]{2,1,0:T(8,128)S(1)} %get-tuple-element.18), kind=kOutput, calls=%fused_computation.30 | convolution fusion | flops 645765120 | bytes 26191872 | tf_op jit(solution)/shard_map/shqk,skhd->sqhd/dot_general | solution.py:88
  381.3 7.8 %convolution_convert_fusion = bf16[16,196,1024]{2,1,0:T(8,128)(2,1)} fusion(bf16[16,196,512]{1,2,0:T(8,128)(2,1)} %bitcast.98, bf16[512,1024]{1,0:T(8,128)(2,1)S(1)} %copy-done.7), kind=kOutput, calls=%fused_computation.13 | convolution fusion | flops 3291545600 | bytes 10682368 | tf_op jit(solution)/shard_map/stc,cd->std/dot_general | solution.py:93
  389.1 0.0 reduce-scatter.2.cloned.1.call-update
  389.1 0.0 all-reduce.4.cloned.1.call-start
  389.2 4.4 gather_fusion.4
  393.6 14.4 %reduce-scatter.2.cloned.1.call-done = bf16[16,196,512]{2,1,0:T(8,128)(2,1)} async-done(((bf16[16,196,1024]{2,1,0:T(8,128)(2,1)}), bf16[16,196,512]{2,1,0:T(8,128)(2,1)}) %reduce-scatter.2.cloned.1.call-update) | async-done | bytes 3211280 | tf_op jit(solution)/shard_map/reduce_scatter | solution.py:94
  408.1 4.8 fusion.2
  412.8 3.5 all-reduce
  416.4 5.2 %fusion.7 = bf16[16,196,256]{2,1,0:T(8,128)(2,1)} fusion(bf16[16,196,512]{2,1,0:T(8,128)(2,1)} %reduce-scatter.2.cloned.1.call-done, f32[16,196]{1,0:T(8,128)S(1)} %get-tuple-element.13, f32[16,196]{1,0:T(8,128)S(1)} %get-tuple-element.12, bf16[512,256]{1,0:T(8,128)(2,1)S(1)} %copy-done.8, bf16[16,196,512]{2,1,0:T(8,128)(2,1)} %gather_fusion.4, ...), kind=kOutput, calls=%fused_computation.35 | convolution fusion | flops 834125824 | bytes 8315408 | tf_op jit(solution)/shard_map/stf,fh->sth/dot_general | solution.py:104
  421.6 0.0 all-reduce.6.cloned.1.call-start
  421.7 0.1 compare_select_fusion.7
  421.8 0.6 gather_fusion.1
  422.4 0.6 gather_fusion.2
  423.7 0.1 reshape.211
  423.8 0.1 dynamic_slice.20
  423.9 25.4 %all-reduce.4.cloned.1.call-done = bf16[16,196,256]{2,1,0:T(8,128)(2,1)} async-done(((bf16[16,196,256]{2,1,0:T(8,128)(2,1)}), bf16[16,196,256]{2,1,0:T(8,128)(2,1)}) %all-reduce.4.cloned.1.call-update) | async-done | bytes 1605648 | tf_op jit(solution)/shard_map/psum | solution.py:103
  449.3 2.4 fusion.25
  451.7 0.1 fusion.93
  451.8 1.0 fusion.23
  452.9 0.3 fusion.24
  453.2 3.5 psum.39
  456.6 0.7 copy.89
  457.3 10.1 %all-to-all-start.2 = ((bf16[64,1,196]{2,1,0:T(2,128)(2,1)}), bf16[64,1,196]{2,1,0:T(2,128)(2,1)S(1)}, u32[]{:S(2)}, u32[]{:S(2)}) async-start(bf16[64,1,196]{2,1,0:T(2,128)(2,1)} %copy.89), calls=%async_computation.3 | async-start | bytes 131072 | tf_op jit(solution)/shard_map/all_to_all | solution.py:137
  467.4 10.3 %all-reduce.6.cloned.1.call-done = bf16[64,1,3,196]{3,0,2,1:T(8,128)(2,1)} async-done(((bf16[64,1,3,196]{3,0,2,1:T(8,128)(2,1)}), bf16[64,1,3,196]{3,0,2,1:T(8,128)(2,1)}) %all-reduce.6.cloned.1.call-update) | async-done | bytes 75280 | tf_op jit(solution)/shard_map/psum | solution.py:130
  477.8 1.6 copy.87
  479.4 10.1 %all-to-all-start.1 = ((bf16[64,1,3,196]{3,2,1,0:T(4,128)(2,1)}), bf16[64,1,3,196]{3,2,1,0:T(4,128)(2,1)S(1)}, u32[]{:S(2)}, u32[]{:S(2)}) async-start(bf16[64,1,3,196]{3,2,1,0:T(4,128)(2,1)} %copy.87), calls=%async_computation.2 | async-start | bytes 262144 | tf_op jit(solution)/shard_map/all_to_all | solution.py:134
  489.5 0.7 broadcast_maximum_fusion
  490.2 8.1 %all-to-all-done.1 = bf16[64,1,3,196]{3,2,1,0:T(4,128)(2,1)S(1)} async-done(((bf16[64,1,3,196]{3,2,1,0:T(4,128)(2,1)}), bf16[64,1,3,196]{3,2,1,0:T(4,128)(2,1)S(1)}, u32[]{:S(2)}, u32[]{:S(2)}) %all-to-all-start.1) | async-done | bytes 75296 | tf_op jit(solution)/shard_map/all_to_all | solution.py:134
  498.3 0.7 convolution_divide_fusion
  (44 shorter events, 0.3 us)
Async XLA Ops:
  7.2 8.3 %copy-start = (bf16[8,196,512]{2,0,1:T(8,128)(2,1)S(1)}, bf16[8,196,512]{2,0,1:T(8,128)(2,1)}, u32[]{:S(2)}) copy-start(bf16[8,196,512]{2,0,1:T(8,128)(2,1)} %param.14) | copy-start | bytes 4816900
  7.2 1.0 copy-start.2
  33.2 218.5 %all-to-all-start = ((bf16[64,1,196,512]{3,2,1,0:T(8,128)(2,1)}), bf16[64,1,196,512]{3,2,1,0:T(8,128)(2,1)}, u32[]{:S(2)}, u32[]{:S(2)}) async-start(bf16[64,1,196,512]{3,2,1,0:T(8,128)(2,1)} %copy.79), calls=%async_computation | async-start | bytes 26214400 | tf_op jit(solution)/shard_map/all_to_all | solution.py:49
  45.4 239.0 %all-gather.2.cloned.1.call-start = ((), (), s32[]{:S(2)}) async-start(), calls=%async_computation.4 | async-start | bytes 9830400 | tf_op jit(solution)/shard_map/all_gather | solution.py:58
  262.9 0.7 copy-start.3
  262.9 21.5 %copy-start.4 = (bf16[1024,512]{1,0:T(8,128)(2,1)S(1)}, bf16[1024,512]{1,0:T(8,128)(2,1)}, u32[]{:S(2)}) copy-start(bf16[1024,512]{1,0:T(8,128)(2,1)} %param.20) | copy-start | bytes 3145732
  263.0 145.1 %reduce-scatter.2.cloned.1.call-start = ((), (), s32[]{:S(2)}) async-start(), calls=%async_computation.5 | async-start | bytes 9830400 | tf_op jit(solution)/shard_map/reduce_scatter | solution.py:94
  292.4 4.5 copy-start.5
  315.4 6.1 %copy-start.6 = (bf16[1024,512]{1,0:T(8,128)(2,1)S(1)}, bf16[1024,512]{1,0:T(8,128)(2,1)}, u32[]{:S(2)}) copy-start(bf16[1024,512]{1,0:T(8,128)(2,1)} %param.19) | copy-start | bytes 3145732
  367.0 14.3 %copy-start.7 = (bf16[512,1024]{1,0:T(8,128)(2,1)S(1)}, bf16[512,1024]{1,0:T(8,128)(2,1)}, u32[]{:S(2)}) copy-start(bf16[512,1024]{1,0:T(8,128)(2,1)} %param.22) | copy-start | bytes 3145732
  389.1 60.2 %all-reduce.4.cloned.1.call-start = ((), (), s32[]{:S(2)}) async-start(), calls=%async_computation.6 | async-start | bytes 3276800 | tf_op jit(solution)/shard_map/psum | solution.py:103
  393.6 22.7 %copy-start.8 = (bf16[512,256]{1,0:T(8,128)(2,1)S(1)}, bf16[512,256]{1,0:T(8,128)(2,1)}, u32[]{:S(2)}) copy-start(bf16[512,256]{1,0:T(8,128)(2,1)} %param.23) | copy-start | bytes 786436
  416.4 33.0 %copy-start.9 = (bf16[256,256]{1,0:T(8,128)(2,1)S(1)}, bf16[256,256]{1,0:T(8,128)(2,1)}, u32[]{:S(2)}) copy-start(bf16[256,256]{1,0:T(8,128)(2,1)} %param.24) | copy-start | bytes 393220
  416.4 33.0 %copy-start.10 = (bf16[4,256]{1,0:T(4,128)(2,1)S(1)}, bf16[4,256]{1,0:T(4,128)(2,1)}, u32[]{:S(2)}) copy-start(bf16[4,256]{1,0:T(4,128)(2,1)} %param.25) | copy-start | bytes 6148
  421.6 56.1 %all-reduce.6.cloned.1.call-start = ((), (), s32[]{:S(2)}) async-start(), calls=%async_computation.7 | async-start | bytes 196608 | tf_op jit(solution)/shard_map/psum | solution.py:130
  423.9 75.2 %copy-start.1 = (bf16[8,196,512]{2,0,1:T(8,128)(2,1)S(1)}, bf16[8,196,512]{2,0,1:T(8,128)(2,1)}, u32[]{:S(2)}) copy-start(bf16[8,196,512]{2,0,1:T(8,128)(2,1)} %param.14) | copy-start | bytes 4816900
  457.3 22.1 %all-to-all-start.2 = ((bf16[64,1,196]{2,1,0:T(2,128)(2,1)}), bf16[64,1,196]{2,1,0:T(2,128)(2,1)S(1)}, u32[]{:S(2)}, u32[]{:S(2)}) async-start(bf16[64,1,196]{2,1,0:T(2,128)(2,1)} %copy.89), calls=%async_computation.3 | async-start | bytes 131072 | tf_op jit(solution)/shard_map/all_to_all | solution.py:137
  479.4 18.9 %all-to-all-start.1 = ((bf16[64,1,3,196]{3,2,1,0:T(4,128)(2,1)}), bf16[64,1,3,196]{3,2,1,0:T(4,128)(2,1)S(1)}, u32[]{:S(2)}, u32[]{:S(2)}) async-start(bf16[64,1,3,196]{3,2,1,0:T(4,128)(2,1)} %copy.87), calls=%async_computation.2 | async-start | bytes 262144 | tf_op jit(solution)/shard_map/all_to_all | solution.py:134
Sparse Core Ops, SparseCore 0:
  263.1 21.3 all-gather.1
  389.3 18.7 reduce-scatter.1
  421.7 27.5 all-reduce.3
  453.0 24.7 all-reduce.5
where the time goes:
time: 507 us; the launch traced here: 506 us
  waiting for transfers between devices  285 us (56%)
  matrix products  80 us (16%)
  local copies, waits for them, and re-layouts  65.9 us (13%)
  starting transfers between devices  32.8 us (6%)
  other arithmetic  20.4 us (4%)
  between operations  14.7 us (3%)
  blocking collectives  6.95 us (1%)
    all_to_all x1, waiting for transfers between devices, local(): lax.all_to_all(outgoing, 'img', split_axis=0, concat_axis=0, tiled=True)  206 us
    psum x1, waiting for transfers between devices, local(): lax.psum(jnp.einsum('stf,fh->sth', normed, head_in, preferred_element_typ...  25.4 us
    all_gather x1, waiting for transfers between devices, local(): shard_piece = lax.all_gather(view_rows, 'mdl', axis=2, tiled=True)  20.5 us
    dot_general x1, matrix products, local(): jnp.einsum('sqhd,skhd->shqk', query_heads, key_heads, preferred_element_t...  17.3 us
    reduce_scatter x1, waiting for transfers between devices, local(): lax.psum_scatter(partial_out.astype(jnp.bfloat16), 'mdl', scatter_dimensi...  14.4 us
    dot_general x1, matrix products, local(): jnp.einsum('shqk,skhd->sqhd', probs, value_heads, preferred_element_type=...  14.3 us
    all_to_all x1, starting transfers between devices, local(): lax.all_to_all(outgoing, 'img', split_axis=0, concat_axis=0, tiled=True)  12.2 us
    convert_element_type x1, local copies, waits for them, and re-layouts, local(): outgoing = jnp.einsum('ntl,lrf->ntrf', select, tokens, preferred_element_...  11.2 us
  transfers between devices with their start and end apart: 7, of which 6 were waited for; matrix products, arithmetic and copies ran while one was open for 2% of the time, Pallas kernels for 0%

commit v1 on v0

v1 whole, which is shorter than its diff:
```python
import functools

import jax
import jax.numpy as jnp
import numpy as np
from jax import lax
from jax.experimental import pallas as pl
from jax.experimental.pallas import tpu as pltpu
from jax.sharding import PartitionSpec as P

D = 1024
HALF = 512
HEAD_DIM = 64
TOK = 196
STEPS = 13
GROUPS = 16
PAD_TOK = STEPS * GROUPS
LANES = 128
BF = jnp.bfloat16
F32 = jnp.float32
MIB = 1 << 20


def spread_kernel(tokens_ref, pairs_ref, perm_ref, out_ref, block):
    for pair_step in range(7):
        if pair_step < 6:
            rows = tokens_ref[:, pair_step * 32 : pair_step * 32 + 32, :]
        else:
            block[...] = jnp.zeros_like(block)
            block[:, 0 : TOK - 192, :] = tokens_ref[:, 192:TOK, :]
            block[:, 16:32, :] = jnp.broadcast_to(pairs_ref[...].reshape(1, 1, HALF), (8, 16, HALF))
            rows = block[...]
        moved = jnp.dot(perm_ref[...], rows.reshape(256, HALF), preferred_element_type=F32)
        moved = moved.astype(BF).reshape(16, 16, HALF)
        for group in range(4):
            out_ref[:, group, pair_step * 16 : pair_step * 16 + 16, :] = moved[
                :, :, group * LANES : (group + 1) * LANES
            ]


def spread(tokens, pair_lanes, perm):
    return pl.pallas_call(
        spread_kernel,
        out_shape=jax.ShapeDtypeStruct((16, 4, 112, LANES), BF),
        scratch_shapes=[pltpu.VMEM((8, 32, HALF), BF)],
        compiler_params=pltpu.CompilerParams(vmem_limit_bytes=32 * MIB),
    )(tokens, pair_lanes, perm)


def select_kernel(pieces_ref, rows_ref, out_ref, images):
    for pair_step in range(7):
        tile = pieces_ref[:, pair_step * 16 : pair_step * 16 + 16, :].astype(F32)
        tile = tile.reshape(64, 2, 8, LANES)
        for half in range(2):
            step = 2 * pair_step + half
            if step < STEPS:
                images[:, step * LANES : (step + 1) * LANES] = (
                    tile[:, half].reshape(512, LANES).astype(BF)
                )
    for part in range(4):
        rows = slice(part * 256, part * 256 + 256)
        hit = rows_ref[rows, :] == lax.broadcasted_iota(jnp.int32, (256, 512), 1)
        chosen = jnp.where(hit, 1.0, 0.0).astype(BF)
        out_ref[rows, :] = jnp.dot(chosen, images[...], preferred_element_type=F32).astype(BF)


def select(pieces, rows):
    return pl.pallas_call(
        select_kernel,
        out_shape=jax.ShapeDtypeStruct((1024, STEPS * LANES), BF),
        scratch_shapes=[pltpu.VMEM((512, STEPS * LANES), BF)],
        compiler_params=pltpu.CompilerParams(vmem_limit_bytes=40 * MIB),
    )(pieces, rows)


def pair_kernel(
    live_ref,
    pieces_ref,
    perm_ref,
    wq0,
    wq1,
    wk0,
    wk1,
    wv0,
    wv1,
    wo0,
    wo1,
    hin0,
    hin1,
    hmid,
    hlast,
    out_ref,
    x_ref,
    q_ref,
    k_ref,
    v_ref,
    att_ref,
):
    pair = pl.program_id(0)

    @pl.when(pair == 0)
    def _():
        for step in range(STEPS):
            lanes = slice(step * LANES, (step + 1) * LANES)
            columns = []
            for core in range(2):
                for group in range(4):
                    tile = pieces_ref[:, group, core, :, lanes].astype(F32)
                    columns.append(tile.reshape(128, LANES).astype(BF))
            rows = jnp.concatenate(columns, axis=1)
            moved = jnp.dot(perm_ref[...], rows, preferred_element_type=F32).astype(BF)
            x_ref[:, step * 16 : step * 16 + 16, :] = moved.reshape(8, 16, D)

    out_ref[...] = jnp.zeros_like(out_ref)

    @pl.when(pair < live_ref[0])
    def _():
        rows = 2 * PAD_TOK
        x = x_ref[pl.ds(2 * pair, 2)].reshape(rows, D)
        for half, (wq, wk, wv) in enumerate(((wq0, wk0, wv0), (wq1, wk1, wv1))):
            cols = slice(half * HALF, (half + 1) * HALF)
            q = jnp.dot(x, wq[...], preferred_element_type=F32).astype(BF)
            q_ref[:, cols] = q * jnp.asarray(HEAD_DIM**-0.5, BF)
            k_ref[:, cols] = jnp.dot(x, wk[...], preferred_element_type=F32).astype(BF)
            v_ref[:, cols] = jnp.dot(x, wv[...], preferred_element_type=F32).astype(BF)

        first = lax.broadcasted_iota(jnp.int32, (PAD_TOK, LANES), 1) < HEAD_DIM
        key_ok = lax.broadcasted_iota(jnp.int32, (rows, PAD_TOK), 1) < TOK

        def heads(index, carry):
            cols = pl.ds(pl.multiple_of(index * LANES, LANES), LANES)
            for slot in range(2):
                mine = slice(slot * PAD_TOK, (slot + 1) * PAD_TOK)
                other = slice((1 - slot) * PAD_TOK, (2 - slot) * PAD_TOK)
                q = q_ref[mine, cols]
                none = jnp.zeros_like(q)
                both = jnp.concatenate([jnp.where(first, q, none), jnp.where(first, none, q)], axis=0)
                scores = lax.dot_general(
                    both, k_ref[other, cols], (((1,), (1,)), ((), ())), preferred_element_type=F32
                )
                scores = jnp.where(key_ok, scores, -jnp.inf)
                weights = jnp.exp(scores - jnp.max(scores, axis=1, keepdims=True))
                probs = weights * (1.0 / jnp.sum(weights, axis=1, keepdims=True))
                got = jnp.dot(probs.astype(BF), v_ref[other, cols], preferred_element_type=F32)
                att_ref[mine, cols] = jnp.where(first, got[:PAD_TOK], got[PAD_TOK:]).astype(BF)
            return carry

        lax.fori_loop(0, D // LANES, heads, 0)

        mixed = x.astype(F32) + jnp.dot(att_ref[:, :HALF], wo0[...], preferred_element_type=F32)
        mixed = mixed + jnp.dot(att_ref[:, HALF:], wo1[...], preferred_element_type=F32)
        mean = jnp.sum(mixed, axis=1, keepdims=True) * (1.0 / D)
        square = jnp.sum(mixed * mixed, axis=1, keepdims=True) * (1.0 / D)
        normed = ((mixed - mean) * lax.rsqrt(square - mean * mean + 1e-05)).astype(BF)
        hidden = jnp.dot(normed[:, :HALF], hin0[...], preferred_element_type=F32)
        hidden = hidden + jnp.dot(normed[:, HALF:], hin1[...], preferred_element_type=F32)
        hidden = jax.nn.gelu(hidden).astype(BF)
        inner = jnp.dot(hidden, hmid[...], preferred_element_type=F32)
        inner = jax.nn.gelu(inner).astype(BF)
        for slot in range(2):
            last = lax.dot_general(
                hlast[...],
                inner[slot * PAD_TOK : (slot + 1) * PAD_TOK],
                (((1,), (1,)), ((), ())),
                preferred_element_type=F32,
            )
            logit = last[3:4, :]
            confidence = 1.0 + jnp.maximum(logit, 0.0) + jnp.log1p(jnp.exp(-jnp.abs(logit)))
            is_conf = lax.broadcasted_iota(jnp.int32, last.shape, 0) == 3
            result = jnp.where(is_conf, 1.0, last) * confidence
            out_ref[slot, :, 0:TOK] = result[:, 0:TOK]


def pair_heads(live, pieces, perm, weights):
    whole = lambda a: pl.BlockSpec(a.shape, lambda i, n=a.ndim: (0,) * n)
    rows = 2 * PAD_TOK
    return pl.pallas_call(
        pair_kernel,
        grid=(4,),
        in_specs=[pl.BlockSpec(memory_space=pltpu.SMEM)] + [whole(a) for a in (pieces, perm, *weights)],
        out_specs=pl.BlockSpec((2, 4, 256), lambda i: (i, 0, 0)),
        out_shape=jax.ShapeDtypeStruct((8, 4, 256), F32),
        scratch_shapes=[
            pltpu.VMEM((8, PAD_TOK, D), BF),
            pltpu.VMEM((rows, D), BF),
            pltpu.VMEM((rows, D), BF),
            pltpu.VMEM((rows, D), BF),
            pltpu.VMEM((rows, D), BF),
        ],
        compiler_params=pltpu.CompilerParams(
            vmem_limit_bytes=56 * MIB, dimension_semantics=("arbitrary",)
        ),
    )(live, pieces, perm, *weights)


def local(
    tokens,
    image_row,
    views,
    pairs,
    pair_count,
    w_query,
    w_key,
    w_value,
    w_out,
    head_in,
    head_mid,
    head_last,
):
    own = lax.axis_index("img")
    core = lax.axis_index("mdl")
    groups = lax.axis_size("img")

    out_row = np.arange(256)
    source = (out_row % 8) * 32 + (out_row // 8 % 2) * 16 + out_row // 16
    spread_perm = jnp.asarray(np.arange(256)[None, :] == source[:, None], BF)
    pair_lanes = jnp.tile(jnp.pad(pairs.reshape(1, 16).astype(BF), ((0, 0), (0, 112))), (1, 4))
    outgoing = spread(tokens, pair_lanes, spread_perm).reshape(64, 112, LANES)
    pieces = lax.all_to_all(outgoing, "img", split_axis=0, concat_axis=0, tiled=True)

    swap = lambda a: lax.ppermute(a, "mdl", [(0, 1), (1, 0)])
    q_other, k_other, v_other, o_other, h_other = (
        swap(a) for a in (w_query, w_key, w_value, w_out, head_in)
    )
    low = core == 0
    hin0 = jnp.where(low, head_in, h_other)
    hin1 = jnp.where(low, h_other, head_in)

    is_image = views[:, :, None] == jnp.arange(image_row.shape[0])
    stored = jnp.sum(jnp.where(is_image, image_row, 0), axis=2)

    all_pairs = pieces[:, 104, :16].astype(jnp.int32)
    is_view = all_pairs[:, :, None] == jnp.arange(16)
    rows = jnp.sum(jnp.where(is_view, stored[:, None, :], 0), axis=2)
    chosen = select(pieces, rows.reshape(1024, 1)).reshape(128, 8, STEPS * LANES)
    arrived = lax.all_to_all(chosen, ("img", "mdl"), split_axis=0, concat_axis=0, tiled=True)

    out_row = np.arange(128)
    source = (out_row % 16) * 8 + out_row // 16
    pair_perm = jnp.asarray(np.arange(128)[None, :] == source[:, None], BF)
    live = jnp.clip(pair_count - 4 * core, 0, 4)
    results = pair_heads(
        live,
        arrived.reshape(GROUPS, 4, 2, 8, STEPS * LANES),
        pair_perm,
        (w_query, q_other, w_key, k_other, w_value, v_other, w_out, o_other, hin0, hin1, head_mid, head_last),
    )

    my_rows = lax.dynamic_index_in_dim(rows, own, 0, keepdims=False)
    my_rows = lax.dynamic_slice_in_dim(my_rows, 8 * core, 8, 0)
    to_owner = (my_rows[None, :] // 8 == jnp.arange(groups)[:, None]).astype(F32)
    sums = jnp.dot(to_owner, results.reshape(8, 1024), precision=lax.Precision.HIGHEST)
    sums = jnp.broadcast_to(sums.astype(BF).reshape(64, 1, 8, LANES), (64, 2, 8, LANES))
    back = lax.all_to_all(
        sums.reshape(128, 8, LANES), ("img", "mdl"), split_axis=0, concat_axis=0, tiled=True
    )
    mine = own * 8 + jnp.arange(8)
    from_pair = jnp.any(stored[None, :, :] == mine[:, None, None], axis=2).astype(BF)
    from_pair = jnp.repeat(from_pair, 2, axis=1)
    total = jnp.dot(from_pair, back.reshape(128, 1024), preferred_element_type=F32)
    total = total.reshape(8, 4, 256)[:, :, :TOK]
    weight_total = total[:, 3]
    joined = total[:, :3] / jnp.maximum(weight_total, 1.0)[:, None, :]
    return (joined, weight_total)


def solution(mesh):
    placed = (
        P("img", None, "mdl"),
        P(),
        P(),
        P("img", None, None),
        P("img"),
        P(None, "mdl"),
        P(None, "mdl"),
        P(None, "mdl"),
        P("mdl", None),
        P("mdl", None),
        P(),
        P(),
    )
    return jax.shard_map(
        local,
        mesh=mesh,
        in_specs=placed,
        out_specs=(P("img", None, None), P("img", None)),
        check_vma=False,
    )
```

time: 507 us -> 179 us (0.35)
  waiting for transfers between devices: 285 us -> 75.1 us
  matrix products: 80 us -> 0.43 us
  local copies, waits for them, and re-layouts: 65.9 us -> 7.59 us
  starting transfers between devices: 32.8 us -> 64.7 us
  Pallas kernels: 0 us -> 24.9 us
  other arithmetic: 20.4 us -> 4.79 us
  between operations: 14.7 us -> 1.49 us
  blocking collectives: 6.95 us -> 0 us
    all_to_all x1, waiting for transfers between devices: 206 us -> 24.3 us  [local(): lax.all_to_all(outgoing, 'img', split_axis=0, concat_axis=0, tiled=True)]
    dot_general x13 -> x2, matrix products: 80 us -> 0.43 us  [the longest x1 0.24 us: local(): jnp.dot(to_owner, results.reshape(8, 1024), precision=lax.Precision.HIGHEST)]
    all_to_all x2, waiting for transfers between devices: 8.06 us -> 44.9 us  [the longest x1 33.9 us: local(): lax.all_to_all(chosen, ('img', 'mdl'), split_axis=0, concat_axis=0, tiled...]
    psum x2 -> x0, waiting for transfers between devices: 35.8 us -> none  [the longest x1 25.4 us: local(): lax.psum(jnp.einsum('stf,fh->sth', normed, head_in, preferred_element_typ...]
    gather x10 -> x0, local copies, waits for them, and re-layouts: 33.1 us -> none  [the longest x1 7.16 us: local(): jnp.take(arriving.reshape(groups * link_cap, tokens_per, quarter), my_own...]
    all_to_all x2, starting transfers between devices: 20.2 us -> 50.4 us  [the longest x1 44 us: local(): lax.all_to_all(sums.reshape(128, 8, LANES), ('img', 'mdl'), split_axis=0,...]
    pallas_call x0 -> x3, Pallas kernels: none -> 24.9 us  [the longest x1 20.2 us: pair_heads(): pl.pallas_call(pair_kernel, grid=(4,), in_specs=[pl.BlockSpec(memory_spac...]
    all_gather x1 -> x0, waiting for transfers between devices: 20.5 us -> none  [local(): shard_piece = lax.all_gather(view_rows, 'mdl', axis=2, tiled=True)]
  transfers between devices with their start and end apart: 7 -> 8, of which waited for: 6 -> 4; matrix products, arithmetic and copies ran while one was open for 2% -> 2% of each run, Pallas kernels for 0% -> 0%
where the time goes in v1:
time: 179 us
  waiting for transfers between devices  75.1 us (42%)
  starting transfers between devices  64.7 us (36%)
  Pallas kernels  24.9 us (14%)
  local copies, waits for them, and re-layouts  7.59 us (4%)
  other arithmetic  4.79 us (3%)
    all_to_all x1, starting transfers between devices, local(): lax.all_to_all(sums.reshape(128, 8, LANES), ('img', 'mdl'), split_axis=0,...  44 us
    all_to_all x1, waiting for transfers between devices, local(): lax.all_to_all(chosen, ('img', 'mdl'), split_axis=0, concat_axis=0, tiled...  33.9 us
    all_to_all x1, waiting for transfers between devices, local(): lax.all_to_all(outgoing, 'img', split_axis=0, concat_axis=0, tiled=True)  24.3 us
    pallas_call x1, Pallas kernels, pair_heads(): pl.pallas_call(pair_kernel, grid=(4,), in_specs=[pl.BlockSpec(memory_spac...  20.2 us
    all_to_all x1, starting transfers between devices, local(): lax.all_to_all(outgoing, 'img', split_axis=0, concat_axis=0, tiled=True)  12.1 us
    all_to_all x1, waiting for transfers between devices, local(): lax.all_to_all(sums.reshape(128, 8, LANES), ('img', 'mdl'), split_axis=0,...  11 us
    all_to_all x1, starting transfers between devices, local(): lax.all_to_all(chosen, ('img', 'mdl'), split_axis=0, concat_axis=0, tiled...  6.44 us
    ppermute x5, waiting for transfers between devices, local(): swap = lambda a: lax.ppermute(a, 'mdl', [(0, 1), (1, 0)])  5.83 us
  transfers between devices with their start and end apart: 8, of which 4 were waited for; matrix products, arithmetic and copies ran while one was open for 2% of the time, Pallas kernels for 0%

profile of v1, /device:TPU:1, one launch (start us, length us, event | category | flops | bytes accessed | tf_op | source)
XLA Modules:
  0.0 179.0 jit_solution(18017997766519872242)
XLA Ops:
  0.6 0.0 copy-start.1
  0.6 0.0 copy-start.5
  0.7 2.0 %copy.41.tokens_ref = bf16[8,196,512]{2,1,0:T(8,128)(2,1)S(1)} copy(bf16[8,196,512]{2,0,1:T(8,128)(2,1)} %param.14) | data formatting | bytes 3211264 | tf_op args[0]
  2.6 0.0 copy-done.5
  2.6 0.1 copy.40
  2.7 0.1 convert_element_type.35
  2.9 0.0 copy-done.1
  2.9 0.6 shard_map.149
  3.5 0.0 copy-start
  3.5 1.2 copy-done
  4.8 0.0 copy-start.3
  4.8 0.0 copy-start.4
  4.8 12.1 %all-to-all-start = ((bf16[64,112,128]{2,1,0:T(8,128)(2,1)}), bf16[64,112,128]{2,1,0:T(8,128)(2,1)S(1)}, u32[]{:S(2)}, u32[]{:S(2)}) async-start(bf16[64,112,128]{2,1,0:T(8,128)(2,1)} %bitcast.34), calls=%async_computation | async-start | bytes 3670016 | tf_op jit(solution)/shard_map/all_to_all | solution.py:219
  16.9 0.0 copy-done.3
  16.9 0.1 copy.37
  17.0 0.0 copy-done.4
  17.0 1.3 select_reduce_fusion
  18.3 0.1 copy.38
  18.3 24.3 %all-to-all-done.pieces_ref = bf16[64,112,128]{2,1,0:T(8,128)(2,1)S(1)} async-done(((bf16[64,112,128]{2,1,0:T(8,128)(2,1)}), bf16[64,112,128]{2,1,0:T(8,128)(2,1)S(1)}, u32[]{:S(2)}, u32[]{:S(2)}) %all-to-all-start) | async-done | bytes 1835040 | tf_op jit(solution)/shard_map/all_to_all | solution.py:219
  42.7 0.1 copy.42
  42.8 0.1 copy.44
  42.9 0.3 reshape.78.rows_ref
  43.2 4.1 %shard_map.150 = bf16[1024,1664]{1,0:T(8,128)(2,1)} custom-call(bf16[64,112,128]{2,1,0:T(8,128)(2,1)S(1)} %all-to-all-done.pieces_ref, s32[1024,1]{1,0:T(8,128)S(1)} %reshape.78.rows_ref), custom_call_target="tpu_custom_call" | custom-call | tf_op jit(solution)/shard_map/pallas_call | solution.py:68
  47.3 6.4 %all-to-all-start.1 = ((bf16[128,8,1664]{2,1,0:T(8,128)(2,1)}), bf16[128,8,1664]{2,1,0:T(8,128)(2,1)S(1)}, u32[]{:S(2)}, u32[]{:S(2)}) async-start(bf16[128,8,1664]{2,1,0:T(8,128)(2,1)} %bitcast.6), calls=%async_computation.1 | async-start | bytes 6815744 | tf_op jit(solution)/shard_map/all_to_all | solution.py:236
  53.8 1.1 collective-permute-start
  54.9 0.1 collective-permute-start.1
  55.0 0.4 collective-permute-start.2
  55.4 0.1 collective-permute-start.3
  55.5 0.4 collective-permute-start.4
  56.6 5.8 %collective-permute-done.4 = bf16[512,256]{1,0:T(8,128)(2,1)} collective-permute-done((bf16[512,256]{1,0:T(8,128)(2,1)}, bf16[512,256]{1,0:T(8,128)(2,1)}, u32[]{:S(2)}, u32[]{:S(2)}) %collective-permute-start.4) | collective-permute-done | bytes 262176 | tf_op jit(solution)/shard_map/ppermute | solution.py:221
  62.4 1.9 %broadcast_select_fusion = (bf16[512,256]{1,0:T(8,128)(2,1)}, bf16[512,256]{1,0:T(8,128)(2,1)}) fusion(bf16[512,256]{1,0:T(8,128)(2,1)} %collective-permute-done.4, bf16[512,256]{1,0:T(8,128)(2,1)} %param.23, pred[]{:T(512)S(6)} %eq.70), kind=kLoop, calls=%fused_computation.4 | loop fusion | flops 262144 | bytes 1048577 | tf_op jit(solution)/shard_map/jit(_where)/select_n | solution.py:227
  64.3 0.2 fusion.3
  64.5 0.0 collective-permute-done.wq1
  64.5 0.0 collective-permute-done.1.wk1
  64.5 0.0 collective-permute-done.2.wv1
  64.5 0.0 collective-permute-done.3.wo1
  64.5 33.9 %all-to-all-done.1 = bf16[128,8,1664]{2,1,0:T(8,128)(2,1)S(1)} async-done(((bf16[128,8,1664]{2,1,0:T(8,128)(2,1)}), bf16[128,8,1664]{2,1,0:T(8,128)(2,1)S(1)}, u32[]{:S(2)}, u32[]{:S(2)}) %all-to-all-start.1) | async-done | bytes 3407904 | tf_op jit(solution)/shard_map/all_to_all | solution.py:236
  98.4 0.0 copy-start.2
  98.4 1.7 copy-done.2
  100.1 20.2 %shard_map.151 = f32[8,4,256]{2,1,0:T(4,128)} custom-call(s32[1]{0:T(128)S(6)} %min.6.live_ref, bf16[16,4,2,8,1664]{4,3,2,1,0:T(8,128)(2,1)} %bitcast.36, bf16[128,128]{1,0:T(8,128)(2,1)} %constant.62.clone.perm_ref, bf16[1024,512]{1,0:T(8,128)(2,1)} %wq0.1, bf16[1024,512]{1,0:T(8,128)(2,1)} %collective-permute-done.wq1, bf16[1024,512]{1,0:T(8,128)(2,1)} %wk0.1, ...), custom_call_target="tpu_custom_call" | custom-call | tf_op jit(solution)/shard_map/pallas_call | solution.py:177
  120.3 0.8 copy.52
  121.1 0.2 fusion
  121.3 0.7 broadcast_in_dim.46
  122.1 44.0 %all-to-all-start.2 = ((bf16[128,8,128]{2,1,0:T(8,128)(2,1)}), bf16[128,8,128]{2,1,0:T(8,128)(2,1)S(1)}, u32[]{:S(2)}, u32[]{:S(2)}) async-start(bf16[128,8,128]{2,1,0:T(8,128)(2,1)} %bitcast.8), calls=%async_computation.2 | async-start | bytes 524288 | tf_op jit(solution)/shard_map/all_to_all | solution.py:254
  166.1 0.1 compare_reduce_fusion
  166.2 0.1 copy.39
  166.3 11.0 %all-to-all-done.2 = bf16[128,8,128]{2,1,0:T(8,128)(2,1)S(1)} async-done(((bf16[128,8,128]{2,1,0:T(8,128)(2,1)}), bf16[128,8,128]{2,1,0:T(8,128)(2,1)S(1)}, u32[]{:S(2)}, u32[]{:S(2)}) %all-to-all-start.2) | async-done | bytes 262176 | tf_op jit(solution)/shard_map/all_to_all | solution.py:254
  177.3 0.2 copy.50
  177.5 0.2 fusion.5
  177.7 0.6 slice_bitcast_fusion
  178.4 0.6 slice_divide_fusion
  (10 shorter events, 0.1 us)
Async XLA Ops:
  0.6 2.2 %copy-start.1 = (bf16[256,256]{1,0:T(8,128)(2,1)S(1)}, bf16[256,256]{1,0:T(8,128)(2,1)}, u32[]{:S(2)}) copy-start(bf16[256,256]{1,0:T(8,128)(2,1)} %constant.61.clone.perm_ref) | copy-start | bytes 393220
  0.6 2.0 %copy-start.5 = (s32[1,8,2]{1,2,0:T(2,128)S(1)}, s32[1,8,2]{1,2,0:T(2,128)}, u32[]{:S(2)}) copy-start(s32[1,8,2]{1,2,0:T(2,128)} %param.17) | copy-start | bytes 196
  3.5 1.2 copy-start
  4.8 12.1 %copy-start.3 = (s32[64,16]{0,1:T(8,128)S(1)}, s32[64,16]{0,1:T(8,128)}, u32[]{:S(2)}) copy-start(s32[64,16]{0,1:T(8,128)} %param.16) | copy-start | bytes 12292
  4.8 12.2 %copy-start.4 = (s32[512]{0:T(512)S(1)}, s32[512]{0:T(512)}, u32[]{:S(2)}) copy-start(s32[512]{0:T(512)} %param.15) | copy-start | bytes 6148
  4.8 37.9 %all-to-all-start = ((bf16[64,112,128]{2,1,0:T(8,128)(2,1)}), bf16[64,112,128]{2,1,0:T(8,128)(2,1)S(1)}, u32[]{:S(2)}, u32[]{:S(2)}) async-start(bf16[64,112,128]{2,1,0:T(8,128)(2,1)} %bitcast.34), calls=%async_computation | async-start | bytes 3670016 | tf_op jit(solution)/shard_map/all_to_all | solution.py:219
  47.3 51.1 %all-to-all-start.1 = ((bf16[128,8,1664]{2,1,0:T(8,128)(2,1)}), bf16[128,8,1664]{2,1,0:T(8,128)(2,1)S(1)}, u32[]{:S(2)}, u32[]{:S(2)}) async-start(bf16[128,8,1664]{2,1,0:T(8,128)(2,1)} %bitcast.6), calls=%async_computation.1 | async-start | bytes 6815744 | tf_op jit(solution)/shard_map/all_to_all | solution.py:236
  53.8 10.7 %collective-permute-start = (bf16[1024,512]{1,0:T(8,128)(2,1)}, bf16[1024,512]{1,0:T(8,128)(2,1)}, u32[]{:S(2)}, u32[]{:S(2)}) collective-permute-start(bf16[1024,512]{1,0:T(8,128)(2,1)} %wq0.1), channel_id=1, source_target_pairs={{0,1},{1,0},{2,3},{3,2},{4,5},{5,4},{6,7},{7,6},{8,9},{9,8},{10,11... | collective-permute-start | bytes 3145736 | tf_op jit(solution)/shard_map/ppermute | solution.py:221
  54.9 9.6 %collective-permute-start.1 = (bf16[1024,512]{1,0:T(8,128)(2,1)}, bf16[1024,512]{1,0:T(8,128)(2,1)}, u32[]{:S(2)}, u32[]{:S(2)}) collective-permute-start(bf16[1024,512]{1,0:T(8,128)(2,1)} %wk0.1), channel_id=1, source_target_pairs={{0,1},{1,0},{2,3},{3,2},{4,5},{5,4},{6,7},{7,6},{8,9},{9,8},{10,11... | collective-permute-start | bytes 3145736 | tf_op jit(solution)/shard_map/ppermute | solution.py:221
  55.0 9.5 %collective-permute-start.2 = (bf16[1024,512]{1,0:T(8,128)(2,1)}, bf16[1024,512]{1,0:T(8,128)(2,1)}, u32[]{:S(2)}, u32[]{:S(2)}) collective-permute-start(bf16[1024,512]{1,0:T(8,128)(2,1)} %wv0.1), channel_id=1, source_target_pairs={{0,1},{1,0},{2,3},{3,2},{4,5},{5,4},{6,7},{7,6},{8,9},{9,8},{10,11... | collective-permute-start | bytes 3145736 | tf_op jit(solution)/shard_map/ppermute | solution.py:221
  55.4 9.1 %collective-permute-start.3 = (bf16[512,1024]{1,0:T(8,128)(2,1)}, bf16[512,1024]{1,0:T(8,128)(2,1)}, u32[]{:S(2)}, u32[]{:S(2)}) collective-permute-start(bf16[512,1024]{1,0:T(8,128)(2,1)} %wo0.1), channel_id=1, source_target_pairs={{0,1},{1,0},{2,3},{3,2},{4,5},{5,4},{6,7},{7,6},{8,9},{9,8},{10,11... | collective-permute-start | bytes 3145736 | tf_op jit(solution)/shard_map/ppermute | solution.py:221
  55.5 6.9 %collective-permute-start.4 = (bf16[512,256]{1,0:T(8,128)(2,1)}, bf16[512,256]{1,0:T(8,128)(2,1)}, u32[]{:S(2)}, u32[]{:S(2)}) collective-permute-start(bf16[512,256]{1,0:T(8,128)(2,1)} %param.23), channel_id=1, source_target_pairs={{0,1},{1,0},{2,3},{3,2},{4,5},{5,4},{6,7},{7,6},{8,9},{9,8},{10,11... | collective-permute-start | bytes 786440 | tf_op jit(solution)/shard_map/ppermute | solution.py:221
  98.4 1.7 copy-start.2
  122.1 55.2 %all-to-all-start.2 = ((bf16[128,8,128]{2,1,0:T(8,128)(2,1)}), bf16[128,8,128]{2,1,0:T(8,128)(2,1)S(1)}, u32[]{:S(2)}, u32[]{:S(2)}) async-start(bf16[128,8,128]{2,1,0:T(8,128)(2,1)} %bitcast.8), calls=%async_computation.2 | async-start | bytes 524288 | tf_op jit(solution)/shard_map/all_to_all | solution.py:254

commit v2 on v1

v2 whole, which is shorter than its diff:
```python
import jax
import jax.numpy as jnp
from jax import lax
from jax.experimental import pallas as pl
from jax.experimental.pallas import tpu as pltpu
from jax.sharding import PartitionSpec as P

D = 1024
HALF = 512
HEAD_DIM = 64
TOK = 196
STEPS = 13
PAD_TOK = 208
ROWS = 2 * PAD_TOK
LANES = 128
AHEAD = 1
BF = jnp.bfloat16
F32 = jnp.float32
MIB = 1 << 20
HBM = pl.BlockSpec(memory_space=pltpu.HBM)
VMEM = pl.BlockSpec(memory_space=pltpu.VMEM)
SMEM = pl.BlockSpec(memory_space=pltpu.SMEM)


def iota(shape, axis):
    return lax.broadcasted_iota(jnp.int32, shape, axis)


def spread_kernel(pairs_ref, tokens_ref, out_ref, tokens, spread_rows, in_sem, out_sem):
    arrive, leave = [], []
    for half in range(2):
        lanes = slice(half * 256, half * 256 + 256)
        arrive.append(
            pltpu.make_async_copy(tokens_ref.at[:, :, lanes], tokens.at[half], in_sem.at[half])
        )
        leave.append(
            pltpu.make_async_copy(
                spread_rows.at[:, 2 * half : 2 * half + 2],
                out_ref.at[:, 2 * half : 2 * half + 2],
                out_sem.at[half],
            )
        )
        arrive[half].start()
    row, high = iota((8, LANES), 0), iota((8, LANES), 1) >= 64
    listed = jnp.zeros((8, LANES), F32)
    for entry in range(16):
        value = pairs_ref[entry % 2, entry // 2].astype(F32)
        place = (row == entry % 8) & (high if entry >= 8 else ~high)
        listed = jnp.where(place, value, listed)
    listed = jnp.broadcast_to(listed.astype(BF)[None, None], (16, 4, 8, LANES))
    spread_rows[:, :, :, STEPS * LANES :] = listed
    left = TOK - 16 * (STEPS - 1)
    spread_rows[left:, :, :, (STEPS - 1) * LANES : STEPS * LANES] = jnp.zeros((16 - left, 4, 8, LANES), BF)
    for half in range(2):
        arrive[half].wait()
        for step in range(STEPS):
            count = min(16, TOK - 16 * step)
            for group in range(2):
                spread_rows[:count, 2 * half + group, :, step * LANES : (step + 1) * LANES] = tokens[
                    half, 16 * step : 16 * step + count, :, group * LANES : (group + 1) * LANES
                ]
        leave[half].start()
    for half in range(2):
        leave[half].wait()


def in_hbm(*arrays):
    return [pltpu.with_memory_space_constraint(a, pltpu.HBM) for a in arrays]


def spread(pairs, tokens):
    shape = (16, 4, 8, 14 * LANES)
    return pl.pallas_call(
        spread_kernel,
        in_specs=[SMEM, HBM],
        out_specs=HBM,
        out_shape=pltpu.HBM(shape, BF),
        scratch_shapes=[
            pltpu.VMEM((2, TOK, 8, 256), BF),
            pltpu.VMEM(shape, BF),
            pltpu.SemaphoreType.DMA((2,)),
            pltpu.SemaphoreType.DMA((2,)),
        ],
        compiler_params=pltpu.CompilerParams(vmem_limit_bytes=24 * MIB),
    )(pairs, *in_hbm(tokens))


def select_kernel(pieces_ref, stored_ref, out_ref, chosen, sems):
    listed = pieces_ref[:, STEPS * LANES :].astype(F32).reshape(64, 8, LANES)
    lane = iota((64, 8, LANES), 2)
    image = jnp.where(listed == (lane & 63).astype(F32), stored_ref[...], 0.0)
    low = jnp.sum(jnp.where(lane < 64, image, 0.0), axis=2, keepdims=True)
    high = jnp.sum(jnp.where(lane < 64, 0.0, image), axis=2, keepdims=True)
    rows = jnp.concatenate([low[:, None], high[:, None]], axis=1).reshape(1024, 1)
    leave = []
    for part in range(4):
        mine = slice(part * 256, part * 256 + 256)
        hit = rows[mine] == iota((256, 512), 1).astype(F32)
        hit = jnp.where(hit, 1.0, 0.0).astype(BF)
        got = jnp.dot(hit, pieces_ref[:, : STEPS * LANES], preferred_element_type=F32)
        chosen[mine, :] = got.astype(BF)
        leave.append(pltpu.make_async_copy(chosen.at[mine], out_ref.at[mine], sems.at[part]))
        leave[part].start()
    for copy in leave:
        copy.wait()


def select(pieces, stored):
    shape = (1024, STEPS * LANES)
    return pl.pallas_call(
        select_kernel,
        in_specs=[VMEM, VMEM],
        out_specs=HBM,
        out_shape=pltpu.HBM(shape, BF),
        scratch_shapes=[pltpu.VMEM(shape, BF), pltpu.SemaphoreType.DMA((4,))],
        compiler_params=pltpu.CompilerParams(vmem_limit_bytes=24 * MIB),
    )(pieces, stored)


def pair_kernel(live_ref, owner_ref, pieces_ref, *refs):
    sources, out_ref = refs[:12], refs[12]
    weights = refs[13:25]
    x_ref, q_ref, k_ref, v_ref, att_ref, total_ref, send_ref, in_sem, out_sem = refs[25:]
    wo0, wo1, hin0, hin1, hmid, hlast = weights[6:]
    arrive = [
        pltpu.make_async_copy(source, weight, in_sem.at[i])
        for i, (source, weight) in enumerate(zip(sources, weights))
    ]
    for copy in arrive:
        copy.start()
    live = live_ref[0]

    out_row = iota((128, 128), 0)
    source = (out_row & 15) * 8 + (out_row >> 4)
    perm = jnp.where(source == iota((128, 128), 1), 1.0, 0.0).astype(BF)
    for step in range(STEPS):
        lanes = slice(step * LANES, (step + 1) * LANES)
        columns = []
        for core in range(2):
            for group in range(4):
                tile = pieces_ref[:, group, core, :, lanes].astype(F32)
                columns.append(tile.reshape(128, LANES).astype(BF))
        moved = jnp.dot(perm, jnp.concatenate(columns, axis=1), preferred_element_type=F32)
        x_ref[:, step * 16 : step * 16 + 16, :] = moved.astype(BF).reshape(8, 16, D)

    total_ref[...] = jnp.zeros_like(total_ref)

    def project(pair, first_use=False):
        x = x_ref[pl.ds(2 * pair, 2)].reshape(ROWS, D)
        for which in range(6):
            half, i = divmod(which, 3)
            cols = slice(half * HALF, (half + 1) * HALF)
            if first_use:
                arrive[which].wait()
            got = jnp.dot(x, weights[which][...], preferred_element_type=F32).astype(BF)
            if i == 0:
                got = got * jnp.asarray(HEAD_DIM**-0.5, BF)
            (q_ref, k_ref, v_ref)[i][:, cols] = got
            yield
        is_pad = iota((16, D), 0) >= TOK - 192
        for slot in range(2):
            tail = slice(slot * PAD_TOK + 192, (slot + 1) * PAD_TOK)
            key = k_ref[slot * PAD_TOK : slot * PAD_TOK + 16, :].astype(F32)[0:1]
            k_ref[tail, :] = jnp.where(is_pad, key, k_ref[tail, :].astype(F32)).astype(BF)

    def attend():
        first = iota((PAD_TOK, LANES), 1) < HEAD_DIM
        ones = jnp.where(iota((PAD_TOK, LANES), 0) < TOK, 1.0, 0.0).astype(BF)
        chains = [
            (
                slice(slot * PAD_TOK, (slot + 1) * PAD_TOK),
                slice((1 - slot) * PAD_TOK, (2 - slot) * PAD_TOK),
                slice(two * LANES, (two + 1) * LANES),
            )
            for two in range(D // LANES)
            for slot in range(2)
        ]
        scores = []
        for turn in range(len(chains) + AHEAD):
            if turn < len(chains):
                mine, other, cols = chains[turn]
                q = q_ref[mine, cols]
                none = jnp.zeros_like(q)
                both = jnp.concatenate([jnp.where(first, q, none), jnp.where(first, none, q)], axis=0)
                scores.append(
                    lax.dot_general(
                        both, k_ref[other, cols], (((1,), (1,)), ((), ())), preferred_element_type=F32
                    )
                )
            if turn >= AHEAD:
                mine, other, cols = chains[turn - AHEAD]
                score = scores[turn - AHEAD]
                weight = jnp.exp(score - jnp.max(score, axis=1, keepdims=True)).astype(BF)
                values = jnp.concatenate([v_ref[other, cols], ones], axis=1)
                got = jnp.dot(weight, values, preferred_element_type=F32)
                top = jnp.where(first, got[:PAD_TOK, :LANES], got[PAD_TOK:, :LANES])
                below = jnp.where(first, got[:PAD_TOK, LANES:], got[PAD_TOK:, LANES:])
                att_ref[mine, cols] = (top / below).astype(BF)

    def head(pair):
        x = x_ref[pl.ds(2 * pair, 2)].reshape(ROWS, D)
        mixed = x.astype(F32) + jnp.dot(att_ref[:, :HALF], wo0[...], preferred_element_type=F32)
        mixed = mixed + jnp.dot(att_ref[:, HALF:], wo1[...], preferred_element_type=F32)
        yield
        mean = jnp.sum(mixed, axis=1, keepdims=True) * (1.0 / D)
        square = jnp.sum(mixed * mixed, axis=1, keepdims=True) * (1.0 / D)
        normed = ((mixed - mean) * lax.rsqrt(square - mean * mean + 1e-05)).astype(BF)
        hidden = jnp.dot(normed[:, :HALF], hin0[...], preferred_element_type=F32)
        hidden = hidden + jnp.dot(normed[:, HALF:], hin1[...], preferred_element_type=F32)
        yield
        hidden = jax.nn.gelu(hidden).astype(BF)
        inner = jnp.dot(hidden, hmid[...], preferred_element_type=F32)
        yield
        inner = jax.nn.gelu(inner).astype(BF)
        for slot in range(2):
            last = lax.dot_general(
                hlast[...],
                inner[slot * PAD_TOK : (slot + 1) * PAD_TOK],
                (((1,), (1,)), ((), ())),
                preferred_element_type=F32,
            )
            logit = last[3:4, :]
            confidence = 1.0 + jnp.maximum(logit, 0.0) + jnp.log1p(jnp.exp(-jnp.abs(logit)))
            result = jnp.where(iota(last.shape, 0) == 3, 1.0, last) * confidence
            owner = owner_ref[2 * pair + slot]
            total_ref[owner, 0:4, :] += result[:, :LANES]
            total_ref[owner, 4:8, 0 : PAD_TOK - LANES] += result[:, LANES:]

    def run(*stages):
        stages = list(stages)
        while stages:
            stages = [stage for stage in stages if next(stage, stages) is None]

    run(project(0, first_use=True))
    attend()
    for copy in arrive[6:]:
        copy.wait()

    def step(pair, carry):
        run(head(pair - 1), project(pair))
        attend()
        return carry

    lax.fori_loop(1, live, step, 0)

    @pl.when(live > 0)
    def _():
        run(head(live - 1))

    send_ref[...] = total_ref[...].astype(BF)
    leave = [pltpu.make_async_copy(send_ref, out_ref.at[:, to], out_sem.at[to]) for to in range(2)]
    for copy in leave:
        copy.start()
    for copy in leave:
        copy.wait()


def pair_heads(live, owners, pieces, weights):
    send = (64, 2, 8, LANES)
    return pl.pallas_call(
        pair_kernel,
        in_specs=[SMEM, SMEM, VMEM] + [HBM] * len(weights),
        out_specs=HBM,
        out_shape=pltpu.HBM(send, BF),
        scratch_shapes=[pltpu.VMEM(a.shape, BF) for a in weights]
        + [pltpu.VMEM((8, PAD_TOK, D), BF)]
        + [pltpu.VMEM((ROWS, D), BF)] * 4
        + [
            pltpu.VMEM((64, 8, LANES), F32),
            pltpu.VMEM((64, 8, LANES), BF),
            pltpu.SemaphoreType.DMA((len(weights),)),
            pltpu.SemaphoreType.DMA((2,)),
        ],
        compiler_params=pltpu.CompilerParams(vmem_limit_bytes=44 * MIB),
    )(live, owners, pieces, *in_hbm(*weights))


def join_kernel(place_ref, back_ref, joined_ref, weight_ref):
    total = jnp.dot(place_ref[...], back_ref[...], preferred_element_type=F32).reshape(8, 8, LANES)
    for start, lanes in ((0, LANES), (4, TOK - LANES)):
        weight = total[start + 3, :, :lanes]
        cols = slice(start * 32, start * 32 + lanes)
        below = jnp.maximum(weight, 1.0)
        for axis in range(3):
            joined_ref[axis, :, cols] = total[start + axis, :, :lanes] / below
        weight_ref[:, cols] = weight


def join(place, back):
    return pl.pallas_call(
        join_kernel,
        in_specs=[VMEM, VMEM],
        out_specs=(VMEM, VMEM),
        out_shape=(
            jax.ShapeDtypeStruct((3, 8, TOK), F32),
            jax.ShapeDtypeStruct((8, TOK), F32),
        ),
        compiler_params=pltpu.CompilerParams(vmem_limit_bytes=8 * MIB),
    )(place, back)


def local(
    tokens,
    image_row,
    views,
    pairs,
    pair_count,
    w_query,
    w_key,
    w_value,
    w_out,
    head_in,
    head_mid,
    head_last,
):
    own = lax.axis_index("img")
    core = lax.axis_index("mdl")

    outgoing = spread(pairs[0].T, tokens.transpose(1, 0, 2)).reshape(64, 8, 14 * LANES)
    pieces = lax.all_to_all(outgoing, "img", split_axis=0, concat_axis=0, tiled=True)

    swap = lambda a: lax.ppermute(a, "mdl", [(0, 1), (1, 0)])
    q_other, k_other, v_other, o_other, h_other = (
        swap(a) for a in (w_query, w_key, w_value, w_out, head_in)
    )
    low = core == 0
    hin0 = jnp.where(low, head_in, h_other)
    hin1 = jnp.where(low, h_other, head_in)

    is_image = views[:, :, None] == jnp.arange(image_row.shape[0])
    stored = jnp.sum(jnp.where(is_image, image_row, 0), axis=2)
    stored_lanes = jnp.pad(stored.astype(F32), ((0, 0), (0, 48)))
    stored_lanes = jnp.concatenate([stored_lanes, stored_lanes], axis=1).reshape(64, 1, LANES)

    chosen = select(pieces.reshape(512, 14 * LANES), stored_lanes)
    arrived = lax.all_to_all(
        chosen.reshape(128, 8, STEPS * LANES),
        ("img", "mdl"),
        split_axis=0,
        concat_axis=0,
        tiled=True,
    )

    my_stored = lax.dynamic_index_in_dim(stored, own, 0, keepdims=False)
    my_views = lax.dynamic_slice_in_dim(pairs.reshape(16), 8 * core, 8, 0)
    my_rows = jnp.sum(jnp.where(my_views[:, None] == jnp.arange(16), my_stored, 0), axis=1)
    live = jnp.clip(pair_count - 4 * core, 0, 4)
    sums = pair_heads(
        live,
        my_rows // 8,
        arrived.reshape(16, 4, 2, 8, STEPS * LANES),
        (w_query, w_key, w_value, q_other, k_other, v_other, w_out, o_other, hin0, hin1, head_mid, head_last),
    )

    back = lax.all_to_all(
        sums.reshape(128, 8, LANES), ("img", "mdl"), split_axis=0, concat_axis=0, tiled=True
    )
    mine = own * 8 + jnp.arange(8)
    named = jnp.any(stored[None, :, :] == mine[:, None, None], axis=2)
    place = jnp.eye(8, dtype=bool)[:, None, None, None, :] & named[None, :, :, None, None]
    place = jnp.broadcast_to(place, (8, 8, 64, 2, 8)).astype(BF).reshape(64, 1024)
    joined, weight_total = join(place, back.reshape(1024, LANES))
    return (joined.transpose(1, 0, 2), weight_total)


def solution(mesh):
    placed = (
        P("img", None, "mdl"),
        P(),
        P(),
        P("img", None, None),
        P("img"),
        P(None, "mdl"),
        P(None, "mdl"),
        P(None, "mdl"),
        P("mdl", None),
        P("mdl", None),
        P(),
        P(),
    )
    return jax.shard_map(
        local,
        mesh=mesh,
        in_specs=placed,
        out_specs=(P("img", None, None), P("img", None)),
        check_vma=False,
    )
```

time: 179 us -> 143 us (0.80)
  starting transfers between devices: 64.7 us -> 37.2 us
  waiting for transfers between devices: 75.1 us -> 69.4 us
    all_to_all x1, starting transfers between devices: 44 us -> 16.6 us  [local(): lax.all_to_all(sums.reshape(128, 8, LANES), ('img', 'mdl'), split_axis=0,...]
    all_to_all x1, waiting for transfers between devices: 11 us -> 5.83 us  [local(): lax.all_to_all(sums.reshape(128, 8, LANES), ('img', 'mdl'), split_axis=0,...]
    unnamed x18 -> x10, local copies, waits for them, and re-layouts: 5.81 us -> 0.86 us
    reshape x2, local copies, waits for them, and re-layouts: 0.52 us -> 3.03 us  [the longest x1 2.95 us: local(): jnp.broadcast_to(place, (8, 8, 64, 2, 8)).astype(BF).reshape(64, 1024)]
    pallas_call x3 -> x4, Pallas kernels: 24.9 us -> 24.8 us  [the longest x1 17.6 us: pair_heads(): pl.pallas_call(pair_kernel, in_specs=[SMEM, SMEM, VMEM] + [HBM] * len(wei...]
  transfers between devices with their start and end apart: 8 -> 8, of which waited for: 4 -> 4; matrix products, arithmetic and copies ran while one was open for 2% -> 7% of each run, Pallas kernels for 0% -> 0%
where the time goes in v2:
time: 143 us
  waiting for transfers between devices  69.4 us (49%)
  starting transfers between devices  37.2 us (26%)
  Pallas kernels  24.8 us (17%)
  local copies, waits for them, and re-layouts  6.09 us (4%)
  other arithmetic  3.91 us (3%)
  between operations  1.46 us (1%)
    all_to_all x1, waiting for transfers between devices, local(): lax.all_to_all(chosen.reshape(128, 8, STEPS * LANES), ('img', 'mdl'), spl...  34.1 us
    all_to_all x1, waiting for transfers between devices, local(): lax.all_to_all(outgoing, 'img', split_axis=0, concat_axis=0, tiled=True)  24.3 us
    pallas_call x1, Pallas kernels, pair_heads(): pl.pallas_call(pair_kernel, in_specs=[SMEM, SMEM, VMEM] + [HBM] * len(wei...  17.6 us
    all_to_all x1, starting transfers between devices, local(): lax.all_to_all(sums.reshape(128, 8, LANES), ('img', 'mdl'), split_axis=0,...  16.6 us
    all_to_all x1, starting transfers between devices, local(): lax.all_to_all(outgoing, 'img', split_axis=0, concat_axis=0, tiled=True)  12 us
    all_to_all x1, starting transfers between devices, local(): lax.all_to_all(chosen.reshape(128, 8, STEPS * LANES), ('img', 'mdl'), spl...  6.46 us
    all_to_all x1, waiting for transfers between devices, local(): lax.all_to_all(sums.reshape(128, 8, LANES), ('img', 'mdl'), split_axis=0,...  5.83 us
    ppermute x5, waiting for transfers between devices, local(): swap = lambda a: lax.ppermute(a, 'mdl', [(0, 1), (1, 0)])  5.21 us
  transfers between devices with their start and end apart: 8, of which 4 were waited for; matrix products, arithmetic and copies ran while one was open for 7% of the time, Pallas kernels for 0%

profile of v2, /device:TPU:1, one launch (start us, length us, event | category | flops | bytes accessed | tf_op | source)
XLA Modules:
  0.0 142.9 jit_solution(6319130680475294115)
XLA Ops:
  0.6 0.0 copy-start
  0.6 0.7 copy-done
  1.3 3.2 %shard_map.131 = bf16[16,4,8,1792]{3,2,1,0:T(8,128)(2,1)} custom-call(s32[2,8]{1,0:T(2,128)S(1)} %bitcast.19, bf16[196,8,512]{2,1,0:T(8,128)(2,1)} %bitcast.22), custom_call_target="tpu_custom_call" | custom-call | tf_op jit(solution)/shard_map/pallas_call | solution.py:73
  4.5 0.0 copy-start.2
  4.5 0.0 copy-start.3
  4.5 12.0 %all-to-all-start = ((bf16[64,8,1792]{2,1,0:T(8,128)(2,1)}), bf16[64,8,1792]{2,1,0:T(8,128)(2,1)S(1)}, u32[]{:S(2)}, u32[]{:S(2)}) async-start(bf16[64,8,1792]{2,1,0:T(8,128)(2,1)} %bitcast.21), calls=%async_computation | async-start | bytes 3670016 | tf_op jit(solution)/shard_map/all_to_all | solution.py:320
  16.5 0.0 copy-done.2
  16.5 0.1 copy.18
  16.6 0.0 copy-done.3
  16.6 1.3 select_reduce_fusion
  17.9 0.1 pad_maximum_fusion
  18.0 24.3 %all-to-all-done = bf16[64,8,1792]{2,1,0:T(8,128)(2,1)S(1)} async-done(((bf16[64,8,1792]{2,1,0:T(8,128)(2,1)}), bf16[64,8,1792]{2,1,0:T(8,128)(2,1)S(1)}, u32[]{:S(2)}, u32[]{:S(2)}) %all-to-all-start) | async-done | bytes 1835040 | tf_op jit(solution)/shard_map/all_to_all | solution.py:320
  42.3 3.2 %shard_map.132 = bf16[1024,1664]{1,0:T(8,128)(2,1)} custom-call(bf16[512,1792]{1,0:T(8,128)(2,1)S(1)} %bitcast.16, f32[64,1,128]{2,1,0:T(1,128)S(1)} %bitcast.18), custom_call_target="tpu_custom_call" | custom-call | tf_op jit(solution)/shard_map/pallas_call | solution.py:110
  45.6 0.0 copy-start.1
  45.6 6.5 %all-to-all-start.1 = ((bf16[128,8,1664]{2,1,0:T(8,128)(2,1)}), bf16[128,8,1664]{2,1,0:T(8,128)(2,1)S(1)}, u32[]{:S(2)}, u32[]{:S(2)}) async-start(bf16[128,8,1664]{2,1,0:T(8,128)(2,1)} %bitcast.20), calls=%async_computation.1 | async-start | bytes 6815744 | tf_op jit(solution)/shard_map/all_to_all | solution.py:336
  52.0 1.1 collective-permute-start
  53.2 0.1 collective-permute-start.1
  53.3 0.4 collective-permute-start.2
  53.7 0.1 collective-permute-start.3
  53.8 0.4 collective-permute-start.4
  54.2 0.0 copy-done.1
  54.2 0.1 copy.20
  54.3 0.1 copy.19
  54.4 0.1 reshape.53
  54.4 0.1 dynamic_slice.7
  54.5 0.2 select_reduce_fusion.1
  54.7 0.1 compare_reduce_fusion
  55.5 5.2 %collective-permute-done.4 = bf16[512,256]{1,0:T(8,128)(2,1)} collective-permute-done((bf16[512,256]{1,0:T(8,128)(2,1)}, bf16[512,256]{1,0:T(8,128)(2,1)}, u32[]{:S(2)}, u32[]{:S(2)}) %collective-permute-start.4) | collective-permute-done | bytes 262176 | tf_op jit(solution)/shard_map/ppermute | solution.py:322
  60.7 1.9 %broadcast_select_fusion = (bf16[512,256]{1,0:T(8,128)(2,1)}, bf16[512,256]{1,0:T(8,128)(2,1)}) fusion(bf16[512,256]{1,0:T(8,128)(2,1)} %collective-permute-done.4, bf16[512,256]{1,0:T(8,128)(2,1)} %param.21, pred[]{:T(512)S(6)} %eq.59), kind=kLoop, calls=%fused_computation.3 | loop fusion | flops 262144 | bytes 1048577 | tf_op jit(solution)/shard_map/jit(_where)/select_n | solution.py:328
  62.6 0.0 collective-permute-done.refs_3_
  62.6 0.0 collective-permute-done.1.refs_4_
  62.6 0.0 collective-permute-done.2.refs_5_
  62.6 0.0 collective-permute-done.3.refs_7_
  62.6 34.1 %all-to-all-done.1 = bf16[128,8,1664]{2,1,0:T(8,128)(2,1)S(1)} async-done(((bf16[128,8,1664]{2,1,0:T(8,128)(2,1)}), bf16[128,8,1664]{2,1,0:T(8,128)(2,1)S(1)}, u32[]{:S(2)}, u32[]{:S(2)}) %all-to-all-start.1) | async-done | bytes 3407904 | tf_op jit(solution)/shard_map/all_to_all | solution.py:336
  96.7 17.6 %shard_map.133 = bf16[64,2,8,128]{3,2,1,0:T(8,128)(2,1)} custom-call(s32[1]{0:T(128)S(6)} %min.6.live_ref, s32[8]{0:T(128)S(1)} %and_select_fusion.owner_ref, bf16[16,4,2,8,1664]{4,3,2,1,0:T(8,128)(2,1)S(1)} %bitcast.15, bf16[1024,512]{1,0:T(8,128)(2,1)} %refs_0_.1, bf16[1024,512]{1,0:T(8,128)(2,1)} %refs_1_.1, bf16[1024,512]{1,0:T(8,128)(2,1)} %refs_2_.1, ...), custom_call_target="tpu_custom_call" | custom-call | tf_op jit(solution)/shard_map/pallas_call | solution.py:260
  114.2 16.6 %all-to-all-start.2 = ((bf16[128,8,128]{2,1,0:T(8,128)(2,1)}), bf16[128,8,128]{2,1,0:T(8,128)(2,1)S(1)}, u32[]{:S(2)}, u32[]{:S(2)}) async-start(bf16[128,8,128]{2,1,0:T(8,128)(2,1)} %bitcast.23), calls=%async_computation.2 | async-start | bytes 524288 | tf_op jit(solution)/shard_map/all_to_all | solution.py:355
  130.8 0.4 and_convert_fusion
  131.2 2.1 %broadcast_in_dim.31 = bf16[8,8,64,2,8]{4,3,2,1,0:T(2,128)(2,1)S(1)} broadcast(bf16[8,8,64,8]{3,2,1,0:T(8,128)(2,1)S(1)} %and_convert_fusion), dimensions={0,1,2,4} | broadcast | bytes 196608 | tf_op jit(solution)/shard_map/broadcast_in_dim | solution.py:361
  133.3 3.0 %reshape.52.place_ref = bf16[64,1024]{1,0:T(8,128)(2,1)S(1)} reshape(bf16[8,8,64,2,8]{4,3,2,1,0:T(2,128)(2,1)S(1)} %broadcast_in_dim.31) | data formatting | bytes 262144 | tf_op jit(solution)/shard_map/reshape | solution.py:361
  136.2 5.8 %all-to-all-done.2 = bf16[128,8,128]{2,1,0:T(8,128)(2,1)S(1)} async-done(((bf16[128,8,128]{2,1,0:T(8,128)(2,1)}), bf16[128,8,128]{2,1,0:T(8,128)(2,1)S(1)}, u32[]{:S(2)}, u32[]{:S(2)}) %all-to-all-start.2) | async-done | bytes 262176 | tf_op jit(solution)/shard_map/all_to_all | solution.py:355
  142.1 0.8 shard_map.134
  (6 shorter events, 0.0 us)
Async XLA Ops:
  0.6 0.7 copy-start
  4.5 12.0 %copy-start.2 = (s32[64,16]{0,1:T(8,128)S(1)}, s32[64,16]{0,1:T(8,128)}, u32[]{:S(2)}) copy-start(s32[64,16]{0,1:T(8,128)} %param.14) | copy-start | bytes 12292
  4.5 12.1 %copy-start.3 = (s32[512]{0:T(512)S(1)}, s32[512]{0:T(512)}, u32[]{:S(2)}) copy-start(s32[512]{0:T(512)} %param.13) | copy-start | bytes 6148
  4.5 37.8 %all-to-all-start = ((bf16[64,8,1792]{2,1,0:T(8,128)(2,1)}), bf16[64,8,1792]{2,1,0:T(8,128)(2,1)S(1)}, u32[]{:S(2)}, u32[]{:S(2)}) async-start(bf16[64,8,1792]{2,1,0:T(8,128)(2,1)} %bitcast.21), calls=%async_computation | async-start | bytes 3670016 | tf_op jit(solution)/shard_map/all_to_all | solution.py:320
  45.6 8.7 %copy-start.1 = (s32[1,8,2]{1,2,0:T(2,128)S(1)}, s32[1,8,2]{1,2,0:T(2,128)}, u32[]{:S(2)}) copy-start(s32[1,8,2]{1,2,0:T(2,128)} %param.15) | copy-start | bytes 196
  45.6 51.1 %all-to-all-start.1 = ((bf16[128,8,1664]{2,1,0:T(8,128)(2,1)}), bf16[128,8,1664]{2,1,0:T(8,128)(2,1)S(1)}, u32[]{:S(2)}, u32[]{:S(2)}) async-start(bf16[128,8,1664]{2,1,0:T(8,128)(2,1)} %bitcast.20), calls=%async_computation.1 | async-start | bytes 6815744 | tf_op jit(solution)/shard_map/all_to_all | solution.py:336
  52.0 10.5 %collective-permute-start = (bf16[1024,512]{1,0:T(8,128)(2,1)}, bf16[1024,512]{1,0:T(8,128)(2,1)}, u32[]{:S(2)}, u32[]{:S(2)}) collective-permute-start(bf16[1024,512]{1,0:T(8,128)(2,1)} %refs_0_.1), channel_id=1, source_target_pairs={{0,1},{1,0},{2,3},{3,2},{4,5},{5,4},{6,7},{7,6},{8,9},{9,8},{10,11... | collective-permute-start | bytes 3145736 | tf_op jit(solution)/shard_map/ppermute | solution.py:322
  53.2 9.4 %collective-permute-start.1 = (bf16[1024,512]{1,0:T(8,128)(2,1)}, bf16[1024,512]{1,0:T(8,128)(2,1)}, u32[]{:S(2)}, u32[]{:S(2)}) collective-permute-start(bf16[1024,512]{1,0:T(8,128)(2,1)} %refs_1_.1), channel_id=1, source_target_pairs={{0,1},{1,0},{2,3},{3,2},{4,5},{5,4},{6,7},{7,6},{8,9},{9,8},{10,11... | collective-permute-start | bytes 3145736 | tf_op jit(solution)/shard_map/ppermute | solution.py:322
  53.3 9.3 %collective-permute-start.2 = (bf16[1024,512]{1,0:T(8,128)(2,1)}, bf16[1024,512]{1,0:T(8,128)(2,1)}, u32[]{:S(2)}, u32[]{:S(2)}) collective-permute-start(bf16[1024,512]{1,0:T(8,128)(2,1)} %refs_2_.1), channel_id=1, source_target_pairs={{0,1},{1,0},{2,3},{3,2},{4,5},{5,4},{6,7},{7,6},{8,9},{9,8},{10,11... | collective-permute-start | bytes 3145736 | tf_op jit(solution)/shard_map/ppermute | solution.py:322
  53.7 8.9 %collective-permute-start.3 = (bf16[512,1024]{1,0:T(8,128)(2,1)}, bf16[512,1024]{1,0:T(8,128)(2,1)}, u32[]{:S(2)}, u32[]{:S(2)}) collective-permute-start(bf16[512,1024]{1,0:T(8,128)(2,1)} %refs_6_.1), channel_id=1, source_target_pairs={{0,1},{1,0},{2,3},{3,2},{4,5},{5,4},{6,7},{7,6},{8,9},{9,8},{10,11... | collective-permute-start | bytes 3145736 | tf_op jit(solution)/shard_map/ppermute | solution.py:322
  53.8 6.9 %collective-permute-start.4 = (bf16[512,256]{1,0:T(8,128)(2,1)}, bf16[512,256]{1,0:T(8,128)(2,1)}, u32[]{:S(2)}, u32[]{:S(2)}) collective-permute-start(bf16[512,256]{1,0:T(8,128)(2,1)} %param.21), channel_id=1, source_target_pairs={{0,1},{1,0},{2,3},{3,2},{4,5},{5,4},{6,7},{7,6},{8,9},{9,8},{10,11... | collective-permute-start | bytes 786440 | tf_op jit(solution)/shard_map/ppermute | solution.py:322
  114.2 27.8 %all-to-all-start.2 = ((bf16[128,8,128]{2,1,0:T(8,128)(2,1)}), bf16[128,8,128]{2,1,0:T(8,128)(2,1)S(1)}, u32[]{:S(2)}, u32[]{:S(2)}) async-start(bf16[128,8,128]{2,1,0:T(8,128)(2,1)} %bitcast.23), calls=%async_computation.2 | async-start | bytes 524288 | tf_op jit(solution)/shard_map/all_to_all | solution.py:355

commit v3 on v2

--- a/solution.py
+++ b/solution.py
@@ -14,6 +14,10 @@
 ROWS = 2 * PAD_TOK
 LANES = 128
 AHEAD = 1
+SELECT_PARTS = ((0, 384), (384, 704), (704, 896), (896, 1024))
+FIRST = 3
+DEPTH = 4
+SPREAD_PARTS = tuple((low, low + 2) for low in range(0, 14, 2))
 BF = jnp.bfloat16
 F32 = jnp.float32
 MIB = 1 << 20
@@ -26,42 +30,45 @@
     return lax.broadcasted_iota(jnp.int32, shape, axis)
 
 
-def spread_kernel(pairs_ref, tokens_ref, out_ref, tokens, spread_rows, in_sem, out_sem):
+def spread_kernel(pairs_ref, tokens_ref, out_ref, pairs, tokens, spread_rows, pairs_sem, in_sem, out_sem):
+    get_pairs = pltpu.make_async_copy(pairs_ref, pairs, pairs_sem)
     arrive, leave = [], []
-    for half in range(2):
-        lanes = slice(half * 256, half * 256 + 256)
-        arrive.append(
-            pltpu.make_async_copy(tokens_ref.at[:, :, lanes], tokens.at[half], in_sem.at[half])
-        )
+    for part, (low, high) in enumerate(SPREAD_PARTS):
+        mine = slice(16 * low, min(16 * high, TOK))
+        arrive.append(pltpu.make_async_copy(tokens_ref.at[mine], tokens.at[mine], in_sem.at[part]))
+        lanes = slice(low * LANES, high * LANES)
         leave.append(
             pltpu.make_async_copy(
-                spread_rows.at[:, 2 * half : 2 * half + 2],
-                out_ref.at[:, 2 * half : 2 * half + 2],
-                out_sem.at[half],
+                spread_rows.at[:, :, :, lanes], out_ref.at[:, :, :, lanes], out_sem.at[part]
             )
         )
-        arrive[half].start()
-    row, high = iota((8, LANES), 0), iota((8, LANES), 1) >= 64
-    listed = jnp.zeros((8, LANES), F32)
-    for entry in range(16):
-        value = pairs_ref[entry % 2, entry // 2].astype(F32)
-        place = (row == entry % 8) & (high if entry >= 8 else ~high)
-        listed = jnp.where(place, value, listed)
-    listed = jnp.broadcast_to(listed.astype(BF)[None, None], (16, 4, 8, LANES))
-    spread_rows[:, :, :, STEPS * LANES :] = listed
-    left = TOK - 16 * (STEPS - 1)
-    spread_rows[left:, :, :, (STEPS - 1) * LANES : STEPS * LANES] = jnp.zeros((16 - left, 4, 8, LANES), BF)
-    for half in range(2):
-        arrive[half].wait()
-        for step in range(STEPS):
+        arrive[part].start()
+    get_pairs.start()
+    for part, (low, high) in enumerate(SPREAD_PARTS):
+        arrive[part].wait()
+        for step in range(low, min(high, STEPS)):
             count = min(16, TOK - 16 * step)
-            for group in range(2):
-                spread_rows[:count, 2 * half + group, :, step * LANES : (step + 1) * LANES] = tokens[
-                    half, 16 * step : 16 * step + count, :, group * LANES : (group + 1) * LANES
+            lanes = slice(step * LANES, (step + 1) * LANES)
+            for group in range(4):
+                spread_rows[:count, group, :, lanes] = tokens[
+                    16 * step : 16 * step + count, :, group * LANES : (group + 1) * LANES
                 ]
-        leave[half].start()
-    for half in range(2):
-        leave[half].wait()
+            if count < 16:
+                spread_rows[count:, :, :, lanes] = jnp.zeros((16 - count, 4, 8, LANES), BF)
+        if high > STEPS:
+            get_pairs.wait()
+            row, upper = iota((8, LANES), 0), iota((8, LANES), 1) >= 64
+            listed = jnp.zeros((8, LANES), F32)
+            for entry in range(16):
+                value = pairs[entry % 2, entry // 2].astype(F32)
+                place = (row == entry % 8) & (upper if entry >= 8 else ~upper)
+                listed = jnp.where(place, value, listed)
+            spread_rows[:, :, :, STEPS * LANES :] = jnp.broadcast_to(
+                listed.astype(BF)[None, None], (16, 4, 8, LANES)
+            )
+        leave[part].start()
+    for copy in leave:
+        copy.wait()
 
 
 def in_hbm(*arrays):
@@ -72,17 +79,19 @@
     shape = (16, 4, 8, 14 * LANES)
     return pl.pallas_call(
         spread_kernel,
-        in_specs=[SMEM, HBM],
+        in_specs=[HBM, HBM],
         out_specs=HBM,
         out_shape=pltpu.HBM(shape, BF),
         scratch_shapes=[
-            pltpu.VMEM((2, TOK, 8, 256), BF),
+            pltpu.SMEM((2, 8), jnp.int32),
+            pltpu.VMEM((TOK, 8, HALF), BF),
             pltpu.VMEM(shape, BF),
-            pltpu.SemaphoreType.DMA((2,)),
-            pltpu.SemaphoreType.DMA((2,)),
+            pltpu.SemaphoreType.DMA,
+            pltpu.SemaphoreType.DMA((len(SPREAD_PARTS),)),
+            pltpu.SemaphoreType.DMA((len(SPREAD_PARTS),)),
         ],
         compiler_params=pltpu.CompilerParams(vmem_limit_bytes=24 * MIB),
-    )(pairs, *in_hbm(tokens))
+    )(*in_hbm(pairs, tokens))
 
 
 def select_kernel(pieces_ref, stored_ref, out_ref, chosen, sems):
@@ -93,9 +102,9 @@
     high = jnp.sum(jnp.where(lane < 64, 0.0, image), axis=2, keepdims=True)
     rows = jnp.concatenate([low[:, None], high[:, None]], axis=1).reshape(1024, 1)
     leave = []
-    for part in range(4):
-        mine = slice(part * 256, part * 256 + 256)
-        hit = rows[mine] == iota((256, 512), 1).astype(F32)
+    for part, (begin, end) in enumerate(SELECT_PARTS):
+        mine = slice(begin, end)
+        hit = rows[mine] == iota((end - begin, 512), 1).astype(F32)
         hit = jnp.where(hit, 1.0, 0.0).astype(BF)
         got = jnp.dot(hit, pieces_ref[:, : STEPS * LANES], preferred_element_type=F32)
         chosen[mine, :] = got.astype(BF)
@@ -112,7 +121,7 @@
         in_specs=[VMEM, VMEM],
         out_specs=HBM,
         out_shape=pltpu.HBM(shape, BF),
-        scratch_shapes=[pltpu.VMEM(shape, BF), pltpu.SemaphoreType.DMA((4,))],
+        scratch_shapes=[pltpu.VMEM(shape, BF), pltpu.SemaphoreType.DMA((len(SELECT_PARTS),))],
         compiler_params=pltpu.CompilerParams(vmem_limit_bytes=24 * MIB),
     )(pieces, stored)
 
@@ -126,7 +135,7 @@
         pltpu.make_async_copy(source, weight, in_sem.at[i])
         for i, (source, weight) in enumerate(zip(sources, weights))
     ]
-    for copy in arrive:
+    for copy in arrive[:FIRST]:
         copy.start()
     live = live_ref[0]
 
@@ -134,6 +143,9 @@
     source = (out_row & 15) * 8 + (out_row >> 4)
     perm = jnp.where(source == iota((128, 128), 1), 1.0, 0.0).astype(BF)
     for step in range(STEPS):
+        if step == STEPS // 2:
+            for copy in arrive[FIRST:DEPTH]:
+                copy.start()
         lanes = slice(step * LANES, (step + 1) * LANES)
         columns = []
         for core in range(2):
@@ -152,6 +164,8 @@
             cols = slice(half * HALF, (half + 1) * HALF)
             if first_use:
                 arrive[which].wait()
+                for copy in arrive[DEPTH + 2 * which : DEPTH + 2 * which + 2]:
+                    copy.start()
             got = jnp.dot(x, weights[which][...], preferred_element_type=F32).astype(BF)
             if i == 0:
                 got = got * jnp.asarray(HEAD_DIM**-0.5, BF)

time: 143 us -> 142 us (level)
  starting transfers between devices: 37.2 us -> 31 us
  Pallas kernels: 24.8 us -> 30.1 us
    pallas_call x1, Pallas kernels: 17.6 us -> 23.8 us  [pair_heads(): pl.pallas_call(pair_kernel, in_specs=[SMEM, SMEM, VMEM] + [HBM] * len(wei...]
    all_to_all x1, starting transfers between devices: 16.6 us -> 10.4 us  [local(): lax.all_to_all(sums.reshape(128, 8, LANES), ('img', 'mdl'), split_axis=0,...]
where the time goes in v3:
time: 142 us; the launch traced here: 141 us
  waiting for transfers between devices  69.4 us (49%)
  starting transfers between devices  31 us (22%)
  Pallas kernels  30.1 us (21%)
  local copies, waits for them, and re-layouts  5.42 us (4%)
  other arithmetic  3.91 us (3%)
  between operations  1.45 us (1%)
    all_to_all x1, waiting for transfers between devices, local(): lax.all_to_all(chosen.reshape(128, 8, STEPS * LANES), ('img', 'mdl'), spl...  34.1 us
    all_to_all x1, waiting for transfers between devices, local(): lax.all_to_all(outgoing, 'img', split_axis=0, concat_axis=0, tiled=True)  24.3 us
    pallas_call x1, Pallas kernels, pair_heads(): pl.pallas_call(pair_kernel, in_specs=[SMEM, SMEM, VMEM] + [HBM] * len(wei...  23.8 us
    all_to_all x1, starting transfers between devices, local(): lax.all_to_all(outgoing, 'img', split_axis=0, concat_axis=0, tiled=True)  12 us
    all_to_all x1, starting transfers between devices, local(): lax.all_to_all(sums.reshape(128, 8, LANES), ('img', 'mdl'), split_axis=0,...  10.4 us
    all_to_all x1, starting transfers between devices, local(): lax.all_to_all(chosen.reshape(128, 8, STEPS * LANES), ('img', 'mdl'), spl...  6.44 us
    all_to_all x1, waiting for transfers between devices, local(): lax.all_to_all(sums.reshape(128, 8, LANES), ('img', 'mdl'), split_axis=0,...  5.83 us
    ppermute x5, waiting for transfers between devices, local(): swap = lambda a: lax.ppermute(a, 'mdl', [(0, 1), (1, 0)])  5.21 us
  transfers between devices with their start and end apart: 8, of which 4 were waited for; matrix products, arithmetic and copies ran while one was open for 7% of the time, Pallas kernels for 0%

profile of v3, /device:TPU:1, one launch (start us, length us, event | category | flops | bytes accessed | tf_op | source)
XLA Modules:
  0.0 141.3 jit_solution(15898012614003510571)
XLA Ops:
  0.6 2.4 %shard_map.131 = bf16[16,4,8,1792]{3,2,1,0:T(8,128)(2,1)} custom-call(s32[2,8]{1,0:T(2,128)} %bitcast.23, bf16[196,8,512]{2,1,0:T(8,128)(2,1)} %bitcast.21), custom_call_target="tpu_custom_call" | custom-call | tf_op jit(solution)/shard_map/pallas_call | solution.py:80
  3.1 0.0 copy-start
  3.1 0.0 copy-start.2
  3.1 12.0 %all-to-all-start = ((bf16[64,8,1792]{2,1,0:T(8,128)(2,1)}), bf16[64,8,1792]{2,1,0:T(8,128)(2,1)S(1)}, u32[]{:S(2)}, u32[]{:S(2)}) async-start(bf16[64,8,1792]{2,1,0:T(8,128)(2,1)} %bitcast.20), calls=%async_computation | async-start | bytes 3670016 | tf_op jit(solution)/shard_map/all_to_all | solution.py:334
  15.1 0.0 copy-done
  15.1 0.1 copy.18
  15.2 0.0 copy-done.2
  15.2 1.3 select_reduce_fusion
  16.5 0.1 pad_maximum_fusion
  16.6 24.3 %all-to-all-done = bf16[64,8,1792]{2,1,0:T(8,128)(2,1)S(1)} async-done(((bf16[64,8,1792]{2,1,0:T(8,128)(2,1)}), bf16[64,8,1792]{2,1,0:T(8,128)(2,1)S(1)}, u32[]{:S(2)}, u32[]{:S(2)}) %all-to-all-start) | async-done | bytes 1835040 | tf_op jit(solution)/shard_map/all_to_all | solution.py:334
  40.9 3.1 %shard_map.132 = bf16[1024,1664]{1,0:T(8,128)(2,1)} custom-call(bf16[512,1792]{1,0:T(8,128)(2,1)S(1)} %bitcast.16, f32[64,1,128]{2,1,0:T(1,128)S(1)} %bitcast.18), custom_call_target="tpu_custom_call" | custom-call | tf_op jit(solution)/shard_map/pallas_call | solution.py:119
  44.0 0.0 copy-start.1
  44.0 6.4 %all-to-all-start.1 = ((bf16[128,8,1664]{2,1,0:T(8,128)(2,1)}), bf16[128,8,1664]{2,1,0:T(8,128)(2,1)S(1)}, u32[]{:S(2)}, u32[]{:S(2)}) async-start(bf16[128,8,1664]{2,1,0:T(8,128)(2,1)} %bitcast.19), calls=%async_computation.1 | async-start | bytes 6815744 | tf_op jit(solution)/shard_map/all_to_all | solution.py:350
  50.5 1.1 collective-permute-start
  51.6 0.1 collective-permute-start.1
  51.7 0.4 collective-permute-start.2
  52.1 0.1 collective-permute-start.3
  52.2 0.4 collective-permute-start.4
  52.6 0.0 copy-done.1
  52.6 0.1 copy.20
  52.7 0.1 copy.19
  52.8 0.1 reshape.53
  52.9 0.1 dynamic_slice.7
  53.0 0.2 select_reduce_fusion.1
  53.1 0.1 compare_reduce_fusion
  53.9 5.2 %collective-permute-done.4 = bf16[512,256]{1,0:T(8,128)(2,1)} collective-permute-done((bf16[512,256]{1,0:T(8,128)(2,1)}, bf16[512,256]{1,0:T(8,128)(2,1)}, u32[]{:S(2)}, u32[]{:S(2)}) %collective-permute-start.4) | collective-permute-done | bytes 262176 | tf_op jit(solution)/shard_map/ppermute | solution.py:336
  59.1 1.9 %broadcast_select_fusion = (bf16[512,256]{1,0:T(8,128)(2,1)}, bf16[512,256]{1,0:T(8,128)(2,1)}) fusion(bf16[512,256]{1,0:T(8,128)(2,1)} %collective-permute-done.4, bf16[512,256]{1,0:T(8,128)(2,1)} %param.21, pred[]{:T(512)S(6)} %eq.59), kind=kLoop, calls=%fused_computation.3 | loop fusion | flops 262144 | bytes 1048577 | tf_op jit(solution)/shard_map/jit(_where)/select_n | solution.py:342
  61.0 0.0 collective-permute-done.refs_3_
  61.0 0.0 collective-permute-done.1.refs_4_
  61.0 0.0 collective-permute-done.2.refs_5_
  61.0 0.0 collective-permute-done.3.refs_7_
  61.0 34.1 %all-to-all-done.1 = bf16[128,8,1664]{2,1,0:T(8,128)(2,1)S(1)} async-done(((bf16[128,8,1664]{2,1,0:T(8,128)(2,1)}), bf16[128,8,1664]{2,1,0:T(8,128)(2,1)S(1)}, u32[]{:S(2)}, u32[]{:S(2)}) %all-to-all-start.1) | async-done | bytes 3407904 | tf_op jit(solution)/shard_map/all_to_all | solution.py:350
  95.1 23.8 %shard_map.133 = bf16[64,2,8,128]{3,2,1,0:T(8,128)(2,1)} custom-call(s32[1]{0:T(128)S(6)} %min.6.live_ref, s32[8]{0:T(128)S(1)} %and_select_fusion.owner_ref, bf16[16,4,2,8,1664]{4,3,2,1,0:T(8,128)(2,1)S(1)} %bitcast.15, bf16[1024,512]{1,0:T(8,128)(2,1)} %refs_0_.1, bf16[1024,512]{1,0:T(8,128)(2,1)} %refs_1_.1, bf16[1024,512]{1,0:T(8,128)(2,1)} %refs_2_.1, ...), custom_call_target="tpu_custom_call" | custom-call | tf_op jit(solution)/shard_map/pallas_call | solution.py:274
  118.9 10.4 %all-to-all-start.2 = ((bf16[128,8,128]{2,1,0:T(8,128)(2,1)}), bf16[128,8,128]{2,1,0:T(8,128)(2,1)S(1)}, u32[]{:S(2)}, u32[]{:S(2)}) async-start(bf16[128,8,128]{2,1,0:T(8,128)(2,1)} %bitcast.22), calls=%async_computation.2 | async-start | bytes 524288 | tf_op jit(solution)/shard_map/all_to_all | solution.py:369
  129.3 0.4 and_convert_fusion
  129.7 2.1 %broadcast_in_dim.31 = bf16[8,8,64,2,8]{4,3,2,1,0:T(2,128)(2,1)S(1)} broadcast(bf16[8,8,64,8]{3,2,1,0:T(8,128)(2,1)S(1)} %and_convert_fusion), dimensions={0,1,2,4} | broadcast | bytes 196608 | tf_op jit(solution)/shard_map/broadcast_in_dim | solution.py:375
  131.8 3.0 %reshape.52.place_ref = bf16[64,1024]{1,0:T(8,128)(2,1)S(1)} reshape(bf16[8,8,64,2,8]{4,3,2,1,0:T(2,128)(2,1)S(1)} %broadcast_in_dim.31) | data formatting | bytes 262144 | tf_op jit(solution)/shard_map/reshape | solution.py:375
  134.7 5.8 %all-to-all-done.2 = bf16[128,8,128]{2,1,0:T(8,128)(2,1)S(1)} async-done(((bf16[128,8,128]{2,1,0:T(8,128)(2,1)}), bf16[128,8,128]{2,1,0:T(8,128)(2,1)S(1)}, u32[]{:S(2)}, u32[]{:S(2)}) %all-to-all-start.2) | async-done | bytes 262176 | tf_op jit(solution)/shard_map/all_to_all | solution.py:369
  140.5 0.8 shard_map.134
  (6 shorter events, 0.0 us)
Async XLA Ops:
  3.1 12.0 %copy-start = (s32[64,16]{0,1:T(8,128)S(1)}, s32[64,16]{0,1:T(8,128)}, u32[]{:S(2)}) copy-start(s32[64,16]{0,1:T(8,128)} %param.14) | copy-start | bytes 12292
  3.1 12.1 %copy-start.2 = (s32[512]{0:T(512)S(1)}, s32[512]{0:T(512)}, u32[]{:S(2)}) copy-start(s32[512]{0:T(512)} %param.13) | copy-start | bytes 6148
  3.1 37.8 %all-to-all-start = ((bf16[64,8,1792]{2,1,0:T(8,128)(2,1)}), bf16[64,8,1792]{2,1,0:T(8,128)(2,1)S(1)}, u32[]{:S(2)}, u32[]{:S(2)}) async-start(bf16[64,8,1792]{2,1,0:T(8,128)(2,1)} %bitcast.20), calls=%async_computation | async-start | bytes 3670016 | tf_op jit(solution)/shard_map/all_to_all | solution.py:334
  44.0 8.6 %copy-start.1 = (s32[1,8,2]{1,2,0:T(2,128)S(1)}, s32[1,8,2]{1,2,0:T(2,128)}, u32[]{:S(2)}) copy-start(s32[1,8,2]{1,2,0:T(2,128)} %param.15) | copy-start | bytes 196
  44.0 51.1 %all-to-all-start.1 = ((bf16[128,8,1664]{2,1,0:T(8,128)(2,1)}), bf16[128,8,1664]{2,1,0:T(8,128)(2,1)S(1)}, u32[]{:S(2)}, u32[]{:S(2)}) async-start(bf16[128,8,1664]{2,1,0:T(8,128)(2,1)} %bitcast.19), calls=%async_computation.1 | async-start | bytes 6815744 | tf_op jit(solution)/shard_map/all_to_all | solution.py:350
  50.5 10.5 %collective-permute-start = (bf16[1024,512]{1,0:T(8,128)(2,1)}, bf16[1024,512]{1,0:T(8,128)(2,1)}, u32[]{:S(2)}, u32[]{:S(2)}) collective-permute-start(bf16[1024,512]{1,0:T(8,128)(2,1)} %refs_0_.1), channel_id=1, source_target_pairs={{0,1},{1,0},{2,3},{3,2},{4,5},{5,4},{6,7},{7,6},{8,9},{9,8},{10,11... | collective-permute-start | bytes 3145736 | tf_op jit(solution)/shard_map/ppermute | solution.py:336
  51.6 9.4 %collective-permute-start.1 = (bf16[1024,512]{1,0:T(8,128)(2,1)}, bf16[1024,512]{1,0:T(8,128)(2,1)}, u32[]{:S(2)}, u32[]{:S(2)}) collective-permute-start(bf16[1024,512]{1,0:T(8,128)(2,1)} %refs_1_.1), channel_id=1, source_target_pairs={{0,1},{1,0},{2,3},{3,2},{4,5},{5,4},{6,7},{7,6},{8,9},{9,8},{10,11... | collective-permute-start | bytes 3145736 | tf_op jit(solution)/shard_map/ppermute | solution.py:336
  51.7 9.3 %collective-permute-start.2 = (bf16[1024,512]{1,0:T(8,128)(2,1)}, bf16[1024,512]{1,0:T(8,128)(2,1)}, u32[]{:S(2)}, u32[]{:S(2)}) collective-permute-start(bf16[1024,512]{1,0:T(8,128)(2,1)} %refs_2_.1), channel_id=1, source_target_pairs={{0,1},{1,0},{2,3},{3,2},{4,5},{5,4},{6,7},{7,6},{8,9},{9,8},{10,11... | collective-permute-start | bytes 3145736 | tf_op jit(solution)/shard_map/ppermute | solution.py:336
  52.1 8.9 %collective-permute-start.3 = (bf16[512,1024]{1,0:T(8,128)(2,1)}, bf16[512,1024]{1,0:T(8,128)(2,1)}, u32[]{:S(2)}, u32[]{:S(2)}) collective-permute-start(bf16[512,1024]{1,0:T(8,128)(2,1)} %refs_6_.1), channel_id=1, source_target_pairs={{0,1},{1,0},{2,3},{3,2},{4,5},{5,4},{6,7},{7,6},{8,9},{9,8},{10,11... | collective-permute-start | bytes 3145736 | tf_op jit(solution)/shard_map/ppermute | solution.py:336
  52.2 6.9 %collective-permute-start.4 = (bf16[512,256]{1,0:T(8,128)(2,1)}, bf16[512,256]{1,0:T(8,128)(2,1)}, u32[]{:S(2)}, u32[]{:S(2)}) collective-permute-start(bf16[512,256]{1,0:T(8,128)(2,1)} %param.21), channel_id=1, source_target_pairs={{0,1},{1,0},{2,3},{3,2},{4,5},{5,4},{6,7},{7,6},{8,9},{9,8},{10,11... | collective-permute-start | bytes 786440 | tf_op jit(solution)/shard_map/ppermute | solution.py:336
  118.9 21.7 %all-to-all-start.2 = ((bf16[128,8,128]{2,1,0:T(8,128)(2,1)}), bf16[128,8,128]{2,1,0:T(8,128)(2,1)S(1)}, u32[]{:S(2)}, u32[]{:S(2)}) async-start(bf16[128,8,128]{2,1,0:T(8,128)(2,1)} %bitcast.22), calls=%async_computation.2 | async-start | bytes 524288 | tf_op jit(solution)/shard_map/all_to_all | solution.py:369

commit v4 on v3

--- a/solution.py
+++ b/solution.py
@@ -14,9 +14,8 @@
 ROWS = 2 * PAD_TOK
 LANES = 128
 AHEAD = 1
+WAITS = {0: (0, 1), 1: (1, 3), 3: (3, 6)}
 SELECT_PARTS = ((0, 384), (384, 704), (704, 896), (896, 1024))
-FIRST = 3
-DEPTH = 4
 SPREAD_PARTS = tuple((low, low + 2) for low in range(0, 14, 2))
 BF = jnp.bfloat16
 F32 = jnp.float32
@@ -126,7 +125,7 @@
     )(pieces, stored)
 
 
-def pair_kernel(live_ref, owner_ref, pieces_ref, *refs):
+def pair_kernel(owner_ref, pieces_ref, *refs):
     sources, out_ref = refs[:12], refs[12]
     weights = refs[13:25]
     x_ref, q_ref, k_ref, v_ref, att_ref, total_ref, send_ref, in_sem, out_sem = refs[25:]
@@ -135,17 +134,13 @@
         pltpu.make_async_copy(source, weight, in_sem.at[i])
         for i, (source, weight) in enumerate(zip(sources, weights))
     ]
-    for copy in arrive[:FIRST]:
+    for copy in arrive[:6]:
         copy.start()
-    live = live_ref[0]
 
     out_row = iota((128, 128), 0)
     source = (out_row & 15) * 8 + (out_row >> 4)
     perm = jnp.where(source == iota((128, 128), 1), 1.0, 0.0).astype(BF)
     for step in range(STEPS):
-        if step == STEPS // 2:
-            for copy in arrive[FIRST:DEPTH]:
-                copy.start()
         lanes = slice(step * LANES, (step + 1) * LANES)
         columns = []
         for core in range(2):
@@ -157,64 +152,75 @@
 
     total_ref[...] = jnp.zeros_like(total_ref)
 
-    def project(pair, first_use=False):
-        x = x_ref[pl.ds(2 * pair, 2)].reshape(ROWS, D)
-        for which in range(6):
+    def project(duo, begin=0, end=6):
+        x = x_ref[4 * duo : 4 * duo + 4].reshape(2 * ROWS, D)
+        for which in range(begin, end):
             half, i = divmod(which, 3)
             cols = slice(half * HALF, (half + 1) * HALF)
-            if first_use:
-                arrive[which].wait()
-                for copy in arrive[DEPTH + 2 * which : DEPTH + 2 * which + 2]:
-                    copy.start()
+            if duo == 0 and which in WAITS:
+                for copy in arrive[slice(*WAITS[which])]:
+                    copy.wait()
+                if which == 1:
+                    for copy in arrive[6:]:
+                        copy.start()
             got = jnp.dot(x, weights[which][...], preferred_element_type=F32).astype(BF)
             if i == 0:
                 got = got * jnp.asarray(HEAD_DIM**-0.5, BF)
-            (q_ref, k_ref, v_ref)[i][:, cols] = got
+            (q_ref, k_ref, v_ref)[i][duo, :, cols] = got
+            if i == 1:
+                is_pad = iota((16, HALF), 0) >= TOK - 192
+                for slot in range(4):
+                    start = slot * PAD_TOK
+                    tail = slice(start + 192, start + PAD_TOK)
+                    key = k_ref[duo, start : start + 16, cols].astype(F32)[0:1]
+                    keys = jnp.where(is_pad, key, k_ref[duo, tail, cols].astype(F32))
+                    k_ref[duo, tail, cols] = keys.astype(BF)
             yield
-        is_pad = iota((16, D), 0) >= TOK - 192
-        for slot in range(2):
-            tail = slice(slot * PAD_TOK + 192, (slot + 1) * PAD_TOK)
-            key = k_ref[slot * PAD_TOK : slot * PAD_TOK + 16, :].astype(F32)[0:1]
-            k_ref[tail, :] = jnp.where(is_pad, key, k_ref[tail, :].astype(F32)).astype(BF)
-
-    def attend():
+
+    def attend(*pairs):
         first = iota((PAD_TOK, LANES), 1) < HEAD_DIM
         ones = jnp.where(iota((PAD_TOK, LANES), 0) < TOK, 1.0, 0.0).astype(BF)
+        block = lambda slot: slice(slot * PAD_TOK, (slot + 1) * PAD_TOK)
         chains = [
             (
-                slice(slot * PAD_TOK, (slot + 1) * PAD_TOK),
-                slice((1 - slot) * PAD_TOK, (2 - slot) * PAD_TOK),
+                pair // 2,
+                block(2 * (pair % 2) + slot),
+                block(2 * (pair % 2) + 1 - slot),
                 slice(two * LANES, (two + 1) * LANES),
             )
+            for pair in pairs
             for two in range(D // LANES)
             for slot in range(2)
         ]
         scores = []
         for turn in range(len(chains) + AHEAD):
             if turn < len(chains):
-                mine, other, cols = chains[turn]
-                q = q_ref[mine, cols]
+                duo, mine, other, cols = chains[turn]
+                q = q_ref[duo, mine, cols]
                 none = jnp.zeros_like(q)
                 both = jnp.concatenate([jnp.where(first, q, none), jnp.where(first, none, q)], axis=0)
                 scores.append(
                     lax.dot_general(
-                        both, k_ref[other, cols], (((1,), (1,)), ((), ())), preferred_element_type=F32
+                        both, k_ref[duo, other, cols], (((1,), (1,)), ((), ())), preferred_element_type=F32
                     )
                 )
             if turn >= AHEAD:
-                mine, other, cols = chains[turn - AHEAD]
+                duo, mine, other, cols = chains[turn - AHEAD]
                 score = scores[turn - AHEAD]
                 weight = jnp.exp(score - jnp.max(score, axis=1, keepdims=True)).astype(BF)
-                values = jnp.concatenate([v_ref[other, cols], ones], axis=1)
+                values = jnp.concatenate([v_ref[duo, other, cols], ones], axis=1)
                 got = jnp.dot(weight, values, preferred_element_type=F32)
                 top = jnp.where(first, got[:PAD_TOK, :LANES], got[PAD_TOK:, :LANES])
                 below = jnp.where(first, got[:PAD_TOK, LANES:], got[PAD_TOK:, LANES:])
-                att_ref[mine, cols] = (top / below).astype(BF)
-
-    def head(pair):
-        x = x_ref[pl.ds(2 * pair, 2)].reshape(ROWS, D)
-        mixed = x.astype(F32) + jnp.dot(att_ref[:, :HALF], wo0[...], preferred_element_type=F32)
-        mixed = mixed + jnp.dot(att_ref[:, HALF:], wo1[...], preferred_element_type=F32)
+                att_ref[duo, mine, cols] = (top / below).astype(BF)
+
+    def head(*pairs):
+        count = 2 * len(pairs)
+        x = x_ref[2 * pairs[0] : 2 * pairs[0] + count].reshape(count * PAD_TOK, D)
+        start = 2 * (pairs[0] % 2) * PAD_TOK
+        att = att_ref.at[pairs[0] // 2, start : start + count * PAD_TOK]
+        mixed = x.astype(F32) + jnp.dot(att[:, :HALF], wo0[...], preferred_element_type=F32)
+        mixed = mixed + jnp.dot(att[:, HALF:], wo1[...], preferred_element_type=F32)
         yield
         mean = jnp.sum(mixed, axis=1, keepdims=True) * (1.0 / D)
         square = jnp.sum(mixed * mixed, axis=1, keepdims=True) * (1.0 / D)
@@ -226,7 +232,7 @@
         inner = jnp.dot(hidden, hmid[...], preferred_element_type=F32)
         yield
         inner = jax.nn.gelu(inner).astype(BF)
-        for slot in range(2):
+        for slot in range(count):
             last = lax.dot_general(
                 hlast[...],
                 inner[slot * PAD_TOK : (slot + 1) * PAD_TOK],
@@ -236,7 +242,7 @@
             logit = last[3:4, :]
             confidence = 1.0 + jnp.maximum(logit, 0.0) + jnp.log1p(jnp.exp(-jnp.abs(logit)))
             result = jnp.where(iota(last.shape, 0) == 3, 1.0, last) * confidence
-            owner = owner_ref[2 * pair + slot]
+            owner = owner_ref[2 * pairs[0] + slot]
             total_ref[owner, 0:4, :] += result[:, :LANES]
             total_ref[owner, 4:8, 0 : PAD_TOK - LANES] += result[:, LANES:]
 
@@ -245,23 +251,16 @@
         while stages:
             stages = [stage for stage in stages if next(stage, stages) is None]
 
-    run(project(0, first_use=True))
-    attend()
+    run(project(0))
+    attend(0)
     for copy in arrive[6:]:
         copy.wait()
-
-    def step(pair, carry):
-        run(head(pair - 1), project(pair))
-        attend()
-        return carry
-
-    lax.fori_loop(1, live, step, 0)
-
-    @pl.when(live > 0)
-    def _():
-        run(head(live - 1))
-
-    send_ref[...] = total_ref[...].astype(BF)
+    run(head(0), project(1, 0, 3))
+    attend(1)
+    run(head(1), project(1, 3, 6))
+    attend(2, 3)
+    run(head(2, 3))
+    send_ref[...] = total_ref[0:64].astype(BF)
     leave = [pltpu.make_async_copy(send_ref, out_ref.at[:, to], out_sem.at[to]) for to in range(2)]
     for copy in leave:
         copy.start()
@@ -269,24 +268,24 @@
         copy.wait()
 
 
-def pair_heads(live, owners, pieces, weights):
+def pair_heads(owners, pieces, weights):
     send = (64, 2, 8, LANES)
     return pl.pallas_call(
         pair_kernel,
-        in_specs=[SMEM, SMEM, VMEM] + [HBM] * len(weights),
+        in_specs=[SMEM, VMEM] + [HBM] * len(weights),
         out_specs=HBM,
         out_shape=pltpu.HBM(send, BF),
         scratch_shapes=[pltpu.VMEM(a.shape, BF) for a in weights]
         + [pltpu.VMEM((8, PAD_TOK, D), BF)]
-        + [pltpu.VMEM((ROWS, D), BF)] * 4
+        + [pltpu.VMEM((2, 2 * ROWS, D), BF)] * 4
         + [
-            pltpu.VMEM((64, 8, LANES), F32),
+            pltpu.VMEM((65, 8, LANES), F32),
             pltpu.VMEM((64, 8, LANES), BF),
             pltpu.SemaphoreType.DMA((len(weights),)),
             pltpu.SemaphoreType.DMA((2,)),
         ],
-        compiler_params=pltpu.CompilerParams(vmem_limit_bytes=44 * MIB),
-    )(live, owners, pieces, *in_hbm(*weights))
+        compiler_params=pltpu.CompilerParams(vmem_limit_bytes=50 * MIB),
+    )(owners, pieces, *in_hbm(*weights))
 
 
 def join_kernel(place_ref, back_ref, joined_ref, weight_ref):
@@ -358,10 +357,9 @@
     my_stored = lax.dynamic_index_in_dim(stored, own, 0, keepdims=False)
     my_views = lax.dynamic_slice_in_dim(pairs.reshape(16), 8 * core, 8, 0)
     my_rows = jnp.sum(jnp.where(my_views[:, None] == jnp.arange(16), my_stored, 0), axis=1)
-    live = jnp.clip(pair_count - 4 * core, 0, 4)
+    live = 4 * core + jnp.arange(8) // 2 < pair_count[0]
     sums = pair_heads(
-        live,
-        my_rows // 8,
+        jnp.where(live, my_rows // 8, 64),
         arrived.reshape(16, 4, 2, 8, STEPS * LANES),
         (w_query, w_key, w_value, q_other, k_other, v_other, w_out, o_other, hin0, hin1, head_mid, head_last),
     )

time: 142 us -> 141 us (level)
  starting transfers between devices: 31 us -> 24.9 us
  Pallas kernels: 30.1 us -> 35.2 us
    all_to_all x1, starting transfers between devices: 10.4 us -> 4.29 us  [local(): lax.all_to_all(sums.reshape(128, 8, LANES), ('img', 'mdl'), split_axis=0,...]
    pallas_call x1, Pallas kernels: 23.8 us -> 28.9 us  [pair_heads(): pl.pallas_call(pair_kernel, in_specs=[SMEM, VMEM] + [HBM] * len(weights),...]
where the time goes in v4:
time: 141 us; the launch traced here: 140 us
  waiting for transfers between devices  69.4 us (49%)
  Pallas kernels  35.2 us (25%)
  starting transfers between devices  24.9 us (18%)
  local copies, waits for them, and re-layouts  5.42 us (4%)
  other arithmetic  3.91 us (3%)
  between operations  1.45 us (1%)
    all_to_all x1, waiting for transfers between devices, local(): lax.all_to_all(chosen.reshape(128, 8, STEPS * LANES), ('img', 'mdl'), spl...  34.1 us
    pallas_call x1, Pallas kernels, pair_heads(): pl.pallas_call(pair_kernel, in_specs=[SMEM, VMEM] + [HBM] * len(weights),...  28.9 us
    all_to_all x1, waiting for transfers between devices, local(): lax.all_to_all(outgoing, 'img', split_axis=0, concat_axis=0, tiled=True)  24.3 us
    all_to_all x1, starting transfers between devices, local(): lax.all_to_all(outgoing, 'img', split_axis=0, concat_axis=0, tiled=True)  12 us
    all_to_all x1, starting transfers between devices, local(): lax.all_to_all(chosen.reshape(128, 8, STEPS * LANES), ('img', 'mdl'), spl...  6.44 us
    all_to_all x1, waiting for transfers between devices, local(): lax.all_to_all(sums.reshape(128, 8, LANES), ('img', 'mdl'), split_axis=0,...  5.83 us
    ppermute x5, waiting for transfers between devices, local(): swap = lambda a: lax.ppermute(a, 'mdl', [(0, 1), (1, 0)])  5.21 us
    all_to_all x1, starting transfers between devices, local(): lax.all_to_all(sums.reshape(128, 8, LANES), ('img', 'mdl'), split_axis=0,...  4.29 us
  transfers between devices with their start and end apart: 8, of which 4 were waited for; matrix products, arithmetic and copies ran while one was open for 7% of the time, Pallas kernels for 0%

profile of v4, /device:TPU:1, one launch (start us, length us, event | category | flops | bytes accessed | tf_op | source)
XLA Modules:
  0.0 140.3 jit_solution(11692541583419854420)
XLA Ops:
  0.6 2.4 %shard_map.131 = bf16[16,4,8,1792]{3,2,1,0:T(8,128)(2,1)} custom-call(s32[2,8]{1,0:T(2,128)} %bitcast.24, bf16[196,8,512]{2,1,0:T(8,128)(2,1)} %bitcast.22), custom_call_target="tpu_custom_call" | custom-call | tf_op jit(solution)/shard_map/pallas_call | solution.py:79
  3.1 0.0 copy-start
  3.1 0.0 copy-start.2
  3.1 12.0 %all-to-all-start = ((bf16[64,8,1792]{2,1,0:T(8,128)(2,1)}), bf16[64,8,1792]{2,1,0:T(8,128)(2,1)S(1)}, u32[]{:S(2)}, u32[]{:S(2)}) async-start(bf16[64,8,1792]{2,1,0:T(8,128)(2,1)} %bitcast.21), calls=%async_computation | async-start | bytes 3670016 | tf_op jit(solution)/shard_map/all_to_all | solution.py:333
  15.1 0.0 copy-done
  15.1 0.1 copy.18
  15.2 0.0 copy-done.2
  15.2 1.3 select_reduce_fusion
  16.5 0.1 pad_maximum_fusion
  16.6 24.3 %all-to-all-done = bf16[64,8,1792]{2,1,0:T(8,128)(2,1)S(1)} async-done(((bf16[64,8,1792]{2,1,0:T(8,128)(2,1)}), bf16[64,8,1792]{2,1,0:T(8,128)(2,1)S(1)}, u32[]{:S(2)}, u32[]{:S(2)}) %all-to-all-start) | async-done | bytes 1835040 | tf_op jit(solution)/shard_map/all_to_all | solution.py:333
  40.9 3.1 %shard_map.132 = bf16[1024,1664]{1,0:T(8,128)(2,1)} custom-call(bf16[512,1792]{1,0:T(8,128)(2,1)S(1)} %bitcast.17, f32[64,1,128]{2,1,0:T(1,128)S(1)} %bitcast.19), custom_call_target="tpu_custom_call" | custom-call | tf_op jit(solution)/shard_map/pallas_call | solution.py:118
  44.0 0.0 copy-start.1
  44.0 6.4 %all-to-all-start.1 = ((bf16[128,8,1664]{2,1,0:T(8,128)(2,1)}), bf16[128,8,1664]{2,1,0:T(8,128)(2,1)S(1)}, u32[]{:S(2)}, u32[]{:S(2)}) async-start(bf16[128,8,1664]{2,1,0:T(8,128)(2,1)} %bitcast.20), calls=%async_computation.1 | async-start | bytes 6815744 | tf_op jit(solution)/shard_map/all_to_all | solution.py:349
  50.5 1.1 collective-permute-start
  51.6 0.1 collective-permute-start.1
  51.7 0.4 collective-permute-start.2
  52.1 0.1 collective-permute-start.3
  52.2 0.4 collective-permute-start.4
  52.6 0.0 copy-done.1
  52.6 0.1 copy.20
  52.7 0.1 copy.19
  52.8 0.1 reshape.53
  52.9 0.1 dynamic_slice.7
  53.0 0.2 select_reduce_fusion.1
  53.1 0.1 compare_reduce_fusion
  53.9 5.2 %collective-permute-done.4 = bf16[512,256]{1,0:T(8,128)(2,1)} collective-permute-done((bf16[512,256]{1,0:T(8,128)(2,1)}, bf16[512,256]{1,0:T(8,128)(2,1)}, u32[]{:S(2)}, u32[]{:S(2)}) %collective-permute-start.4) | collective-permute-done | bytes 262176 | tf_op jit(solution)/shard_map/ppermute | solution.py:335
  59.1 1.9 %broadcast_select_fusion = (bf16[512,256]{1,0:T(8,128)(2,1)}, bf16[512,256]{1,0:T(8,128)(2,1)}) fusion(bf16[512,256]{1,0:T(8,128)(2,1)} %collective-permute-done.4, bf16[512,256]{1,0:T(8,128)(2,1)} %param.21, pred[]{:T(512)S(6)} %eq.59), kind=kLoop, calls=%fused_computation.3 | loop fusion | flops 262144 | bytes 1048577 | tf_op jit(solution)/shard_map/jit(_where)/select_n | solution.py:341
  61.0 0.0 collective-permute-done.refs_3_
  61.0 0.0 collective-permute-done.1.refs_4_
  61.0 0.0 collective-permute-done.2.refs_5_
  61.0 0.0 collective-permute-done.3.refs_7_
  61.0 34.1 %all-to-all-done.1 = bf16[128,8,1664]{2,1,0:T(8,128)(2,1)S(1)} async-done(((bf16[128,8,1664]{2,1,0:T(8,128)(2,1)}), bf16[128,8,1664]{2,1,0:T(8,128)(2,1)S(1)}, u32[]{:S(2)}, u32[]{:S(2)}) %all-to-all-start.1) | async-done | bytes 3407904 | tf_op jit(solution)/shard_map/all_to_all | solution.py:349
  95.1 28.9 %shard_map.133 = bf16[64,2,8,128]{3,2,1,0:T(8,128)(2,1)} custom-call(s32[8]{0:T(128)S(1)} %compare_select_fusion.owner_ref, bf16[16,4,2,8,1664]{4,3,2,1,0:T(8,128)(2,1)S(1)} %bitcast.16, bf16[1024,512]{1,0:T(8,128)(2,1)} %refs_0_.1, bf16[1024,512]{1,0:T(8,128)(2,1)} %refs_1_.1, bf16[1024,512]{1,0:T(8,128)(2,1)} %refs_2_.1, ...), custom_call_target="tpu_custom_call" | custom-call | tf_op jit(solution)/shard_map/pallas_call | solution.py:273
  124.0 4.3 %all-to-all-start.2 = ((bf16[128,8,128]{2,1,0:T(8,128)(2,1)}), bf16[128,8,128]{2,1,0:T(8,128)(2,1)S(1)}, u32[]{:S(2)}, u32[]{:S(2)}) async-start(bf16[128,8,128]{2,1,0:T(8,128)(2,1)} %bitcast.23), calls=%async_computation.2 | async-start | bytes 524288 | tf_op jit(solution)/shard_map/all_to_all | solution.py:367
  128.3 0.4 and_convert_fusion
  128.7 2.1 %broadcast_in_dim.35 = bf16[8,8,64,2,8]{4,3,2,1,0:T(2,128)(2,1)S(1)} broadcast(bf16[8,8,64,8]{3,2,1,0:T(8,128)(2,1)S(1)} %and_convert_fusion), dimensions={0,1,2,4} | broadcast | bytes 196608 | tf_op jit(solution)/shard_map/broadcast_in_dim | solution.py:373
  130.7 3.0 %reshape.52.place_ref = bf16[64,1024]{1,0:T(8,128)(2,1)S(1)} reshape(bf16[8,8,64,2,8]{4,3,2,1,0:T(2,128)(2,1)S(1)} %broadcast_in_dim.35) | data formatting | bytes 262144 | tf_op jit(solution)/shard_map/reshape | solution.py:373
  133.7 5.8 %all-to-all-done.2 = bf16[128,8,128]{2,1,0:T(8,128)(2,1)S(1)} async-done(((bf16[128,8,128]{2,1,0:T(8,128)(2,1)}), bf16[128,8,128]{2,1,0:T(8,128)(2,1)S(1)}, u32[]{:S(2)}, u32[]{:S(2)}) %all-to-all-start.2) | async-done | bytes 262176 | tf_op jit(solution)/shard_map/all_to_all | solution.py:367
  139.5 0.8 shard_map.134
  (6 shorter events, 0.0 us)
Async XLA Ops:
  3.1 12.0 %copy-start = (s32[64,16]{0,1:T(8,128)S(1)}, s32[64,16]{0,1:T(8,128)}, u32[]{:S(2)}) copy-start(s32[64,16]{0,1:T(8,128)} %param.14) | copy-start | bytes 12292
  3.1 12.1 %copy-start.2 = (s32[512]{0:T(512)S(1)}, s32[512]{0:T(512)}, u32[]{:S(2)}) copy-start(s32[512]{0:T(512)} %param.13) | copy-start | bytes 6148
  3.1 37.8 %all-to-all-start = ((bf16[64,8,1792]{2,1,0:T(8,128)(2,1)}), bf16[64,8,1792]{2,1,0:T(8,128)(2,1)S(1)}, u32[]{:S(2)}, u32[]{:S(2)}) async-start(bf16[64,8,1792]{2,1,0:T(8,128)(2,1)} %bitcast.21), calls=%async_computation | async-start | bytes 3670016 | tf_op jit(solution)/shard_map/all_to_all | solution.py:333
  44.0 8.6 %copy-start.1 = (s32[1,8,2]{1,2,0:T(2,128)S(1)}, s32[1,8,2]{1,2,0:T(2,128)}, u32[]{:S(2)}) copy-start(s32[1,8,2]{1,2,0:T(2,128)} %param.15) | copy-start | bytes 196
  44.0 51.1 %all-to-all-start.1 = ((bf16[128,8,1664]{2,1,0:T(8,128)(2,1)}), bf16[128,8,1664]{2,1,0:T(8,128)(2,1)S(1)}, u32[]{:S(2)}, u32[]{:S(2)}) async-start(bf16[128,8,1664]{2,1,0:T(8,128)(2,1)} %bitcast.20), calls=%async_computation.1 | async-start | bytes 6815744 | tf_op jit(solution)/shard_map/all_to_all | solution.py:349
  50.5 10.5 %collective-permute-start = (bf16[1024,512]{1,0:T(8,128)(2,1)}, bf16[1024,512]{1,0:T(8,128)(2,1)}, u32[]{:S(2)}, u32[]{:S(2)}) collective-permute-start(bf16[1024,512]{1,0:T(8,128)(2,1)} %refs_0_.1), channel_id=1, source_target_pairs={{0,1},{1,0},{2,3},{3,2},{4,5},{5,4},{6,7},{7,6},{8,9},{9,8},{10,11... | collective-permute-start | bytes 3145736 | tf_op jit(solution)/shard_map/ppermute | solution.py:335
  51.6 9.4 %collective-permute-start.1 = (bf16[1024,512]{1,0:T(8,128)(2,1)}, bf16[1024,512]{1,0:T(8,128)(2,1)}, u32[]{:S(2)}, u32[]{:S(2)}) collective-permute-start(bf16[1024,512]{1,0:T(8,128)(2,1)} %refs_1_.1), channel_id=1, source_target_pairs={{0,1},{1,0},{2,3},{3,2},{4,5},{5,4},{6,7},{7,6},{8,9},{9,8},{10,11... | collective-permute-start | bytes 3145736 | tf_op jit(solution)/shard_map/ppermute | solution.py:335
  51.7 9.3 %collective-permute-start.2 = (bf16[1024,512]{1,0:T(8,128)(2,1)}, bf16[1024,512]{1,0:T(8,128)(2,1)}, u32[]{:S(2)}, u32[]{:S(2)}) collective-permute-start(bf16[1024,512]{1,0:T(8,128)(2,1)} %refs_2_.1), channel_id=1, source_target_pairs={{0,1},{1,0},{2,3},{3,2},{4,5},{5,4},{6,7},{7,6},{8,9},{9,8},{10,11... | collective-permute-start | bytes 3145736 | tf_op jit(solution)/shard_map/ppermute | solution.py:335
  52.1 8.9 %collective-permute-start.3 = (bf16[512,1024]{1,0:T(8,128)(2,1)}, bf16[512,1024]{1,0:T(8,128)(2,1)}, u32[]{:S(2)}, u32[]{:S(2)}) collective-permute-start(bf16[512,1024]{1,0:T(8,128)(2,1)} %refs_6_.1), channel_id=1, source_target_pairs={{0,1},{1,0},{2,3},{3,2},{4,5},{5,4},{6,7},{7,6},{8,9},{9,8},{10,11... | collective-permute-start | bytes 3145736 | tf_op jit(solution)/shard_map/ppermute | solution.py:335
  52.2 6.9 %collective-permute-start.4 = (bf16[512,256]{1,0:T(8,128)(2,1)}, bf16[512,256]{1,0:T(8,128)(2,1)}, u32[]{:S(2)}, u32[]{:S(2)}) collective-permute-start(bf16[512,256]{1,0:T(8,128)(2,1)} %param.21), channel_id=1, source_target_pairs={{0,1},{1,0},{2,3},{3,2},{4,5},{5,4},{6,7},{7,6},{8,9},{9,8},{10,11... | collective-permute-start | bytes 786440 | tf_op jit(solution)/shard_map/ppermute | solution.py:335
  124.0 15.5 %all-to-all-start.2 = ((bf16[128,8,128]{2,1,0:T(8,128)(2,1)}), bf16[128,8,128]{2,1,0:T(8,128)(2,1)S(1)}, u32[]{:S(2)}, u32[]{:S(2)}) async-start(bf16[128,8,128]{2,1,0:T(8,128)(2,1)} %bitcast.23), calls=%async_computation.2 | async-start | bytes 524288 | tf_op jit(solution)/shard_map/all_to_all | solution.py:367

commit v5 on v4

--- a/solution.py
+++ b/solution.py
@@ -14,9 +14,10 @@
 ROWS = 2 * PAD_TOK
 LANES = 128
 AHEAD = 1
+BODY = 12 * LANES
 WAITS = {0: (0, 1), 1: (1, 3), 3: (3, 6)}
 SELECT_PARTS = ((0, 384), (384, 704), (704, 896), (896, 1024))
-SPREAD_PARTS = tuple((low, low + 2) for low in range(0, 14, 2))
+SPREAD_PARTS = tuple((low, min(low + 2, STEPS)) for low in range(0, STEPS, 2))
 BF = jnp.bfloat16
 F32 = jnp.float32
 MIB = 1 << 20
@@ -45,26 +46,28 @@
     get_pairs.start()
     for part, (low, high) in enumerate(SPREAD_PARTS):
         arrive[part].wait()
-        for step in range(low, min(high, STEPS)):
-            count = min(16, TOK - 16 * step)
+        for step in range(low, min(high, STEPS - 1)):
             lanes = slice(step * LANES, (step + 1) * LANES)
             for group in range(4):
-                spread_rows[:count, group, :, lanes] = tokens[
-                    16 * step : 16 * step + count, :, group * LANES : (group + 1) * LANES
+                spread_rows[:, group, :, lanes] = tokens[
+                    16 * step : 16 * step + 16, :, group * LANES : (group + 1) * LANES
                 ]
-            if count < 16:
-                spread_rows[count:, :, :, lanes] = jnp.zeros((16 - count, 4, 8, LANES), BF)
-        if high > STEPS:
+        if high == STEPS:
             get_pairs.wait()
-            row, upper = iota((8, LANES), 0), iota((8, LANES), 1) >= 64
-            listed = jnp.zeros((8, LANES), F32)
+            row, place = iota((8, HALF), 0), (iota((8, HALF), 1) >> 5) & 3
+            listed = [jnp.zeros((8, HALF), F32)] * 2
             for entry in range(16):
                 value = pairs[entry % 2, entry // 2].astype(F32)
-                place = (row == entry % 8) & (upper if entry >= 8 else ~upper)
-                listed = jnp.where(place, value, listed)
-            spread_rows[:, :, :, STEPS * LANES :] = jnp.broadcast_to(
-                listed.astype(BF)[None, None], (16, 4, 8, LANES)
-            )
+                listed[entry // 8] = jnp.where(row == entry % 8, value, listed[entry // 8])
+            lanes = slice((STEPS - 1) * LANES, STEPS * LANES)
+            for group in range(16):
+                token, block = divmod(group, 4)
+                last = jnp.where(place == (block + 2) % 4, listed[1], 0.0)
+                last = jnp.where(place == (block + 1) % 4, listed[0], last)
+                last = jnp.where(place == block, tokens[16 * (STEPS - 1) + token].astype(F32), last)
+                last = last.astype(BF)
+                for feature in range(4):
+                    spread_rows[group, feature, :, lanes] = last[:, feature * LANES : (feature + 1) * LANES]
         leave[part].start()
     for copy in leave:
         copy.wait()
@@ -75,7 +78,7 @@
 
 
 def spread(pairs, tokens):
-    shape = (16, 4, 8, 14 * LANES)
+    shape = (16, 4, 8, STEPS * LANES)
     return pl.pallas_call(
         spread_kernel,
         in_specs=[HBM, HBM],
@@ -93,36 +96,42 @@
     )(*in_hbm(pairs, tokens))
 
 
-def select_kernel(pieces_ref, stored_ref, out_ref, chosen, sems):
-    listed = pieces_ref[:, STEPS * LANES :].astype(F32).reshape(64, 8, LANES)
+def select_kernel(block_ref, pieces_ref, stored_ref, out_ref, chosen, sems):
+    block = block_ref[0]
+    last = pieces_ref[:, BODY:]
+    listed = last.astype(F32).reshape(64, 8, LANES)
     lane = iota((64, 8, LANES), 2)
-    image = jnp.where(listed == (lane & 63).astype(F32), stored_ref[...], 0.0)
-    low = jnp.sum(jnp.where(lane < 64, image, 0.0), axis=2, keepdims=True)
-    high = jnp.sum(jnp.where(lane < 64, 0.0, image), axis=2, keepdims=True)
+    place = (lane >> 5) & 3
+    image = jnp.where(listed == (lane & 31).astype(F32), stored_ref[...], 0.0)
+    low = jnp.sum(jnp.where(place == ((block + 1) & 3), image, 0.0), axis=2, keepdims=True)
+    high = jnp.sum(jnp.where(place == ((block + 2) & 3), image, 0.0), axis=2, keepdims=True)
+    is_token = (iota((512, LANES), 1) >> 5) == block
+    last = jnp.where(is_token, last.astype(F32), 0.0).astype(BF)
     rows = jnp.concatenate([low[:, None], high[:, None]], axis=1).reshape(1024, 1)
     leave = []
     for part, (begin, end) in enumerate(SELECT_PARTS):
         mine = slice(begin, end)
         hit = rows[mine] == iota((end - begin, 512), 1).astype(F32)
         hit = jnp.where(hit, 1.0, 0.0).astype(BF)
-        got = jnp.dot(hit, pieces_ref[:, : STEPS * LANES], preferred_element_type=F32)
-        chosen[mine, :] = got.astype(BF)
+        got = jnp.dot(hit, pieces_ref[:, :BODY], preferred_element_type=F32)
+        chosen[mine, :BODY] = got.astype(BF)
+        chosen[mine, BODY:] = jnp.dot(hit, last, preferred_element_type=F32).astype(BF)
         leave.append(pltpu.make_async_copy(chosen.at[mine], out_ref.at[mine], sems.at[part]))
         leave[part].start()
     for copy in leave:
         copy.wait()
 
 
-def select(pieces, stored):
+def select(block, pieces, stored):
     shape = (1024, STEPS * LANES)
     return pl.pallas_call(
         select_kernel,
-        in_specs=[VMEM, VMEM],
+        in_specs=[SMEM, VMEM, VMEM],
         out_specs=HBM,
         out_shape=pltpu.HBM(shape, BF),
         scratch_shapes=[pltpu.VMEM(shape, BF), pltpu.SemaphoreType.DMA((len(SELECT_PARTS),))],
         compiler_params=pltpu.CompilerParams(vmem_limit_bytes=24 * MIB),
-    )(pieces, stored)
+    )(block, pieces, stored)
 
 
 def pair_kernel(owner_ref, pieces_ref, *refs):
@@ -139,7 +148,10 @@
 
     out_row = iota((128, 128), 0)
     source = (out_row & 15) * 8 + (out_row >> 4)
-    perm = jnp.where(source == iota((128, 128), 1), 1.0, 0.0).astype(BF)
+    in_row = iota((128, 128), 1)
+    perm = jnp.where(source == in_row, 1.0, 0.0).astype(BF)
+    is_part = ((in_row & 7) == (out_row >> 4)) & ((in_row >> 5) == (out_row & 15))
+    perm_last = jnp.where(is_part, 1.0, 0.0).astype(BF)
     for step in range(STEPS):
         lanes = slice(step * LANES, (step + 1) * LANES)
         columns = []
@@ -147,7 +159,8 @@
             for group in range(4):
                 tile = pieces_ref[:, group, core, :, lanes].astype(F32)
                 columns.append(tile.reshape(128, LANES).astype(BF))
-        moved = jnp.dot(perm, jnp.concatenate(columns, axis=1), preferred_element_type=F32)
+        order = perm if step < STEPS - 1 else perm_last
+        moved = jnp.dot(order, jnp.concatenate(columns, axis=1), preferred_element_type=F32)
         x_ref[:, step * 16 : step * 16 + 16, :] = moved.astype(BF).reshape(8, 16, D)
 
     total_ref[...] = jnp.zeros_like(total_ref)
@@ -259,7 +272,7 @@
     attend(1)
     run(head(1), project(1, 3, 6))
     attend(2, 3)
-    run(head(2, 3))
+    run(head(2), head(3))
     send_ref[...] = total_ref[0:64].astype(BF)
     leave = [pltpu.make_async_copy(send_ref, out_ref.at[:, to], out_sem.at[to]) for to in range(2)]
     for copy in leave:
@@ -329,7 +342,7 @@
     own = lax.axis_index("img")
     core = lax.axis_index("mdl")
 
-    outgoing = spread(pairs[0].T, tokens.transpose(1, 0, 2)).reshape(64, 8, 14 * LANES)
+    outgoing = spread(pairs[0].T, tokens.transpose(1, 0, 2)).reshape(64, 8, STEPS * LANES)
     pieces = lax.all_to_all(outgoing, "img", split_axis=0, concat_axis=0, tiled=True)
 
     swap = lambda a: lax.ppermute(a, "mdl", [(0, 1), (1, 0)])
@@ -342,10 +355,11 @@
 
     is_image = views[:, :, None] == jnp.arange(image_row.shape[0])
     stored = jnp.sum(jnp.where(is_image, image_row, 0), axis=2)
-    stored_lanes = jnp.pad(stored.astype(F32), ((0, 0), (0, 48)))
-    stored_lanes = jnp.concatenate([stored_lanes, stored_lanes], axis=1).reshape(64, 1, LANES)
-
-    chosen = select(pieces.reshape(512, 14 * LANES), stored_lanes)
+    stored_lanes = jnp.pad(stored.astype(F32), ((0, 0), (0, 16)))
+    stored_lanes = jnp.tile(stored_lanes, (1, 4)).reshape(64, 1, LANES)
+
+    block = (own // 4 % 4).reshape(1)
+    chosen = select(block, pieces.reshape(512, STEPS * LANES), stored_lanes)
     arrived = lax.all_to_all(
         chosen.reshape(128, 8, STEPS * LANES),
         ("img", "mdl"),

time: 141 us -> 139 us (0.986)
    all_to_all x1, waiting for transfers between devices: 24.3 us -> 22.8 us  [local(): lax.all_to_all(outgoing, 'img', split_axis=0, concat_axis=0, tiled=True)]
where the time goes in v5:
time: 139 us; the launch traced here: 138 us
  waiting for transfers between devices  68 us (49%)
  Pallas kernels  34.6 us (25%)
  starting transfers between devices  24.7 us (18%)
  local copies, waits for them, and re-layouts  5.56 us (4%)
  other arithmetic  3.83 us (3%)
  between operations  1.48 us (1%)
    all_to_all x1, waiting for transfers between devices, local(): lax.all_to_all(chosen.reshape(128, 8, STEPS * LANES), ('img', 'mdl'), spl...  34.1 us
    pallas_call x1, Pallas kernels, pair_heads(): pl.pallas_call(pair_kernel, in_specs=[SMEM, VMEM] + [HBM] * len(weights),...  28.3 us
    all_to_all x1, waiting for transfers between devices, local(): lax.all_to_all(outgoing, 'img', split_axis=0, concat_axis=0, tiled=True)  22.8 us
    all_to_all x1, starting transfers between devices, local(): lax.all_to_all(outgoing, 'img', split_axis=0, concat_axis=0, tiled=True)  12 us
    all_to_all x1, starting transfers between devices, local(): lax.all_to_all(chosen.reshape(128, 8, STEPS * LANES), ('img', 'mdl'), spl...  6.26 us
    all_to_all x1, waiting for transfers between devices, local(): lax.all_to_all(sums.reshape(128, 8, LANES), ('img', 'mdl'), split_axis=0,...  5.83 us
    ppermute x5, waiting for transfers between devices, local(): swap = lambda a: lax.ppermute(a, 'mdl', [(0, 1), (1, 0)])  5.21 us
    all_to_all x1, starting transfers between devices, local(): lax.all_to_all(sums.reshape(128, 8, LANES), ('img', 'mdl'), split_axis=0,...  4.31 us
  transfers between devices with their start and end apart: 8, of which 4 were waited for; matrix products, arithmetic and copies ran while one was open for 7% of the time, Pallas kernels for 0%

profile of v5, /device:TPU:1, one launch (start us, length us, event | category | flops | bytes accessed | tf_op | source)
XLA Modules:
  0.0 138.2 jit_solution(7485681818592901250)
XLA Ops:
  0.6 2.4 %shard_map.131 = bf16[16,4,8,1664]{3,2,1,0:T(8,128)(2,1)} custom-call(s32[2,8]{1,0:T(2,128)} %bitcast.25, bf16[196,8,512]{2,1,0:T(8,128)(2,1)} %bitcast.22), custom_call_target="tpu_custom_call" | custom-call | tf_op jit(solution)/shard_map/pallas_call | solution.py:82
  3.0 0.0 copy-start
  3.0 0.0 copy-start.2
  3.0 12.0 %all-to-all-start = ((bf16[64,8,1664]{2,1,0:T(8,128)(2,1)}), bf16[64,8,1664]{2,1,0:T(8,128)(2,1)S(1)}, u32[]{:S(2)}, u32[]{:S(2)}) async-start(bf16[64,8,1664]{2,1,0:T(8,128)(2,1)} %bitcast.21), calls=%async_computation | async-start | bytes 3407872 | tf_op jit(solution)/shard_map/all_to_all | solution.py:346
  15.0 0.0 copy-done
  15.0 0.1 copy.20
  15.1 0.0 copy-done.2
  15.1 1.3 select_reduce_fusion
  16.4 0.1 copy.25
  16.5 0.1 copy.24.stored_ref
  16.6 22.8 %all-to-all-done = bf16[64,8,1664]{2,1,0:T(8,128)(2,1)S(1)} async-done(((bf16[64,8,1664]{2,1,0:T(8,128)(2,1)}), bf16[64,8,1664]{2,1,0:T(8,128)(2,1)S(1)}, u32[]{:S(2)}, u32[]{:S(2)}) %all-to-all-start) | async-done | bytes 1703968 | tf_op jit(solution)/shard_map/all_to_all | solution.py:346
  39.4 3.1 %shard_map.132 = bf16[1024,1664]{1,0:T(8,128)(2,1)} custom-call(s32[1]{0:T(128)} %bitcast.2.block_ref, bf16[512,1664]{1,0:T(8,128)(2,1)S(1)} %bitcast.18, f32[64,1,128]{2,1,0:T(1,128)S(1)} %copy.24.stored_ref), custom_call_target="tpu_custom_call" | custom-call | tf_op jit(solution)/shard_map/pallas_call | solution.py:127
  42.6 0.0 copy-start.1
  42.6 6.3 %all-to-all-start.1 = ((bf16[128,8,1664]{2,1,0:T(8,128)(2,1)}), bf16[128,8,1664]{2,1,0:T(8,128)(2,1)S(1)}, u32[]{:S(2)}, u32[]{:S(2)}) async-start(bf16[128,8,1664]{2,1,0:T(8,128)(2,1)} %bitcast.20), calls=%async_computation.1 | async-start | bytes 6815744 | tf_op jit(solution)/shard_map/all_to_all | solution.py:363
  48.8 1.1 collective-permute-start
  50.0 0.1 collective-permute-start.1
  50.1 0.4 collective-permute-start.2
  50.5 0.1 collective-permute-start.3
  50.6 0.4 collective-permute-start.4
  51.0 0.0 copy-done.1
  51.0 0.1 copy.22
  51.1 0.1 copy.21
  51.1 0.1 reshape.59
  51.2 0.1 dynamic_slice.7
  51.3 0.2 select_reduce_fusion.1
  51.5 0.1 compare_reduce_fusion
  52.3 5.2 %collective-permute-done.4 = bf16[512,256]{1,0:T(8,128)(2,1)} collective-permute-done((bf16[512,256]{1,0:T(8,128)(2,1)}, bf16[512,256]{1,0:T(8,128)(2,1)}, u32[]{:S(2)}, u32[]{:S(2)}) %collective-permute-start.4) | collective-permute-done | bytes 262176 | tf_op jit(solution)/shard_map/ppermute | solution.py:348
  57.5 1.9 %broadcast_select_fusion = (bf16[512,256]{1,0:T(8,128)(2,1)}, bf16[512,256]{1,0:T(8,128)(2,1)}) fusion(bf16[512,256]{1,0:T(8,128)(2,1)} %collective-permute-done.4, bf16[512,256]{1,0:T(8,128)(2,1)} %param.21, pred[]{:T(512)S(6)} %eq.61), kind=kLoop, calls=%fused_computation.3 | loop fusion | flops 262144 | bytes 1048577 | tf_op jit(solution)/shard_map/jit(_where)/select_n | solution.py:354
  59.3 0.0 collective-permute-done.refs_3_
  59.3 0.0 collective-permute-done.1.refs_4_
  59.3 0.0 collective-permute-done.2.refs_5_
  59.3 0.0 collective-permute-done.3.refs_7_
  59.4 34.1 %all-to-all-done.1 = bf16[128,8,1664]{2,1,0:T(8,128)(2,1)S(1)} async-done(((bf16[128,8,1664]{2,1,0:T(8,128)(2,1)}), bf16[128,8,1664]{2,1,0:T(8,128)(2,1)S(1)}, u32[]{:S(2)}, u32[]{:S(2)}) %all-to-all-start.1) | async-done | bytes 3407904 | tf_op jit(solution)/shard_map/all_to_all | solution.py:363
  93.5 28.3 %shard_map.133 = bf16[64,2,8,128]{3,2,1,0:T(8,128)(2,1)} custom-call(s32[8]{0:T(128)S(1)} %compare_select_fusion.owner_ref, bf16[16,4,2,8,1664]{4,3,2,1,0:T(8,128)(2,1)S(1)} %bitcast.17, bf16[1024,512]{1,0:T(8,128)(2,1)} %refs_0_.1, bf16[1024,512]{1,0:T(8,128)(2,1)} %refs_1_.1, bf16[1024,512]{1,0:T(8,128)(2,1)} %refs_2_.1, ...), custom_call_target="tpu_custom_call" | custom-call | tf_op jit(solution)/shard_map/pallas_call | solution.py:286
  121.8 4.3 %all-to-all-start.2 = ((bf16[128,8,128]{2,1,0:T(8,128)(2,1)}), bf16[128,8,128]{2,1,0:T(8,128)(2,1)S(1)}, u32[]{:S(2)}, u32[]{:S(2)}) async-start(bf16[128,8,128]{2,1,0:T(8,128)(2,1)} %bitcast.23), calls=%async_computation.2 | async-start | bytes 524288 | tf_op jit(solution)/shard_map/all_to_all | solution.py:381
  126.1 0.4 and_convert_fusion
  126.5 2.1 %broadcast_in_dim.35 = bf16[8,8,64,2,8]{4,3,2,1,0:T(2,128)(2,1)S(1)} broadcast(bf16[8,8,64,8]{3,2,1,0:T(8,128)(2,1)S(1)} %and_convert_fusion), dimensions={0,1,2,4} | broadcast | bytes 196608 | tf_op jit(solution)/shard_map/broadcast_in_dim | solution.py:387
  128.6 3.0 %reshape.58.place_ref = bf16[64,1024]{1,0:T(8,128)(2,1)S(1)} reshape(bf16[8,8,64,2,8]{4,3,2,1,0:T(2,128)(2,1)S(1)} %broadcast_in_dim.35) | data formatting | bytes 262144 | tf_op jit(solution)/shard_map/reshape | solution.py:387
  131.5 5.8 %all-to-all-done.2 = bf16[128,8,128]{2,1,0:T(8,128)(2,1)S(1)} async-done(((bf16[128,8,128]{2,1,0:T(8,128)(2,1)}), bf16[128,8,128]{2,1,0:T(8,128)(2,1)S(1)}, u32[]{:S(2)}, u32[]{:S(2)}) %all-to-all-start.2) | async-done | bytes 262176 | tf_op jit(solution)/shard_map/all_to_all | solution.py:381
  137.4 0.8 shard_map.134
  (7 shorter events, 0.0 us)
Async XLA Ops:
  3.0 12.0 %copy-start = (s32[64,16]{0,1:T(8,128)S(1)}, s32[64,16]{0,1:T(8,128)}, u32[]{:S(2)}) copy-start(s32[64,16]{0,1:T(8,128)} %param.14) | copy-start | bytes 12292
  3.0 12.1 %copy-start.2 = (s32[512]{0:T(512)S(1)}, s32[512]{0:T(512)}, u32[]{:S(2)}) copy-start(s32[512]{0:T(512)} %param.13) | copy-start | bytes 6148
  3.0 36.4 %all-to-all-start = ((bf16[64,8,1664]{2,1,0:T(8,128)(2,1)}), bf16[64,8,1664]{2,1,0:T(8,128)(2,1)S(1)}, u32[]{:S(2)}, u32[]{:S(2)}) async-start(bf16[64,8,1664]{2,1,0:T(8,128)(2,1)} %bitcast.21), calls=%async_computation | async-start | bytes 3407872 | tf_op jit(solution)/shard_map/all_to_all | solution.py:346
  42.6 8.5 %copy-start.1 = (s32[1,8,2]{1,2,0:T(2,128)S(1)}, s32[1,8,2]{1,2,0:T(2,128)}, u32[]{:S(2)}) copy-start(s32[1,8,2]{1,2,0:T(2,128)} %param.15) | copy-start | bytes 196
  42.6 50.9 %all-to-all-start.1 = ((bf16[128,8,1664]{2,1,0:T(8,128)(2,1)}), bf16[128,8,1664]{2,1,0:T(8,128)(2,1)S(1)}, u32[]{:S(2)}, u32[]{:S(2)}) async-start(bf16[128,8,1664]{2,1,0:T(8,128)(2,1)} %bitcast.20), calls=%async_computation.1 | async-start | bytes 6815744 | tf_op jit(solution)/shard_map/all_to_all | solution.py:363
  48.8 10.5 %collective-permute-start = (bf16[1024,512]{1,0:T(8,128)(2,1)}, bf16[1024,512]{1,0:T(8,128)(2,1)}, u32[]{:S(2)}, u32[]{:S(2)}) collective-permute-start(bf16[1024,512]{1,0:T(8,128)(2,1)} %refs_0_.1), channel_id=1, source_target_pairs={{0,1},{1,0},{2,3},{3,2},{4,5},{5,4},{6,7},{7,6},{8,9},{9,8},{10,11... | collective-permute-start | bytes 3145736 | tf_op jit(solution)/shard_map/ppermute | solution.py:348
  50.0 9.4 %collective-permute-start.1 = (bf16[1024,512]{1,0:T(8,128)(2,1)}, bf16[1024,512]{1,0:T(8,128)(2,1)}, u32[]{:S(2)}, u32[]{:S(2)}) collective-permute-start(bf16[1024,512]{1,0:T(8,128)(2,1)} %refs_1_.1), channel_id=1, source_target_pairs={{0,1},{1,0},{2,3},{3,2},{4,5},{5,4},{6,7},{7,6},{8,9},{9,8},{10,11... | collective-permute-start | bytes 3145736 | tf_op jit(solution)/shard_map/ppermute | solution.py:348
  50.1 9.3 %collective-permute-start.2 = (bf16[1024,512]{1,0:T(8,128)(2,1)}, bf16[1024,512]{1,0:T(8,128)(2,1)}, u32[]{:S(2)}, u32[]{:S(2)}) collective-permute-start(bf16[1024,512]{1,0:T(8,128)(2,1)} %refs_2_.1), channel_id=1, source_target_pairs={{0,1},{1,0},{2,3},{3,2},{4,5},{5,4},{6,7},{7,6},{8,9},{9,8},{10,11... | collective-permute-start | bytes 3145736 | tf_op jit(solution)/shard_map/ppermute | solution.py:348
  50.5 8.9 %collective-permute-start.3 = (bf16[512,1024]{1,0:T(8,128)(2,1)}, bf16[512,1024]{1,0:T(8,128)(2,1)}, u32[]{:S(2)}, u32[]{:S(2)}) collective-permute-start(bf16[512,1024]{1,0:T(8,128)(2,1)} %refs_6_.1), channel_id=1, source_target_pairs={{0,1},{1,0},{2,3},{3,2},{4,5},{5,4},{6,7},{7,6},{8,9},{9,8},{10,11... | collective-permute-start | bytes 3145736 | tf_op jit(solution)/shard_map/ppermute | solution.py:348
  50.6 6.9 %collective-permute-start.4 = (bf16[512,256]{1,0:T(8,128)(2,1)}, bf16[512,256]{1,0:T(8,128)(2,1)}, u32[]{:S(2)}, u32[]{:S(2)}) collective-permute-start(bf16[512,256]{1,0:T(8,128)(2,1)} %param.21), channel_id=1, source_target_pairs={{0,1},{1,0},{2,3},{3,2},{4,5},{5,4},{6,7},{7,6},{8,9},{9,8},{10,11... | collective-permute-start | bytes 786440 | tf_op jit(solution)/shard_map/ppermute | solution.py:348
  121.8 15.5 %all-to-all-start.2 = ((bf16[128,8,128]{2,1,0:T(8,128)(2,1)}), bf16[128,8,128]{2,1,0:T(8,128)(2,1)S(1)}, u32[]{:S(2)}, u32[]{:S(2)}) async-start(bf16[128,8,128]{2,1,0:T(8,128)(2,1)} %bitcast.23), calls=%async_computation.2 | async-start | bytes 524288 | tf_op jit(solution)/shard_map/all_to_all | solution.py:381

commit v6 on v5

--- a/solution.py
+++ b/solution.py
@@ -1,5 +1,6 @@
 import jax
 import jax.numpy as jnp
+import numpy as np
 from jax import lax
 from jax.experimental import pallas as pl
 from jax.experimental.pallas import tpu as pltpu
@@ -28,6 +29,11 @@
 
 def iota(shape, axis):
     return lax.broadcasted_iota(jnp.int32, shape, axis)
+
+
+def gelu(x):
+    root = (2.0 / np.pi) ** 0.5
+    return (0.5 * x) * (1.0 + jnp.tanh(x * (root + (0.044715 * root) * (x * x))))
 
 
 def spread_kernel(pairs_ref, tokens_ref, out_ref, pairs, tokens, spread_rows, pairs_sem, in_sem, out_sem):
@@ -241,10 +247,10 @@
         hidden = jnp.dot(normed[:, :HALF], hin0[...], preferred_element_type=F32)
         hidden = hidden + jnp.dot(normed[:, HALF:], hin1[...], preferred_element_type=F32)
         yield
-        hidden = jax.nn.gelu(hidden).astype(BF)
+        hidden = gelu(hidden).astype(BF)
         inner = jnp.dot(hidden, hmid[...], preferred_element_type=F32)
         yield
-        inner = jax.nn.gelu(inner).astype(BF)
+        inner = gelu(inner).astype(BF)
         for slot in range(count):
             last = lax.dot_general(
                 hlast[...],

time: 139 us -> 139 us (level)
  no operation moved by 1% of the time
where the time goes in v6:
time: 139 us; the launch traced here: 138 us
  waiting for transfers between devices  68 us (49%)
  Pallas kernels  34.6 us (25%)
  starting transfers between devices  24.7 us (18%)
  local copies, waits for them, and re-layouts  5.56 us (4%)
  other arithmetic  3.83 us (3%)
  between operations  1.48 us (1%)
    all_to_all x1, waiting for transfers between devices, local(): lax.all_to_all(chosen.reshape(128, 8, STEPS * LANES), ('img', 'mdl'), spl...  34.1 us
    pallas_call x1, Pallas kernels, pair_heads(): pl.pallas_call(pair_kernel, in_specs=[SMEM, VMEM] + [HBM] * len(weights),...  28.3 us
    all_to_all x1, waiting for transfers between devices, local(): lax.all_to_all(outgoing, 'img', split_axis=0, concat_axis=0, tiled=True)  22.8 us
    all_to_all x1, starting transfers between devices, local(): lax.all_to_all(outgoing, 'img', split_axis=0, concat_axis=0, tiled=True)  12 us
    all_to_all x1, starting transfers between devices, local(): lax.all_to_all(chosen.reshape(128, 8, STEPS * LANES), ('img', 'mdl'), spl...  6.26 us
    all_to_all x1, waiting for transfers between devices, local(): lax.all_to_all(sums.reshape(128, 8, LANES), ('img', 'mdl'), split_axis=0,...  5.83 us
    ppermute x5, waiting for transfers between devices, local(): swap = lambda a: lax.ppermute(a, 'mdl', [(0, 1), (1, 0)])  5.21 us
    all_to_all x1, starting transfers between devices, local(): lax.all_to_all(sums.reshape(128, 8, LANES), ('img', 'mdl'), split_axis=0,...  4.3 us
  transfers between devices with their start and end apart: 8, of which 4 were waited for; matrix products, arithmetic and copies ran while one was open for 7% of the time, Pallas kernels for 0%

profile of v6, /device:TPU:1, one launch (start us, length us, event | category | flops | bytes accessed | tf_op | source)
XLA Modules:
  0.0 138.1 jit_solution(9534739712938266102)
XLA Ops:
  0.6 2.4 %shard_map.131 = bf16[16,4,8,1664]{3,2,1,0:T(8,128)(2,1)} custom-call(s32[2,8]{1,0:T(2,128)} %bitcast.25, bf16[196,8,512]{2,1,0:T(8,128)(2,1)} %bitcast.22), custom_call_target="tpu_custom_call" | custom-call | tf_op jit(solution)/shard_map/pallas_call | solution.py:88
  3.0 0.0 copy-start
  3.0 0.0 copy-start.2
  3.0 12.0 %all-to-all-start = ((bf16[64,8,1664]{2,1,0:T(8,128)(2,1)}), bf16[64,8,1664]{2,1,0:T(8,128)(2,1)S(1)}, u32[]{:S(2)}, u32[]{:S(2)}) async-start(bf16[64,8,1664]{2,1,0:T(8,128)(2,1)} %bitcast.21), calls=%async_computation | async-start | bytes 3407872 | tf_op jit(solution)/shard_map/all_to_all | solution.py:352
  15.0 0.0 copy-done
  15.0 0.1 copy.20
  15.1 0.0 copy-done.2
  15.1 1.3 select_reduce_fusion
  16.4 0.1 copy.25
  16.5 0.1 copy.24.stored_ref
  16.6 22.8 %all-to-all-done = bf16[64,8,1664]{2,1,0:T(8,128)(2,1)S(1)} async-done(((bf16[64,8,1664]{2,1,0:T(8,128)(2,1)}), bf16[64,8,1664]{2,1,0:T(8,128)(2,1)S(1)}, u32[]{:S(2)}, u32[]{:S(2)}) %all-to-all-start) | async-done | bytes 1703968 | tf_op jit(solution)/shard_map/all_to_all | solution.py:352
  39.4 3.1 %shard_map.132 = bf16[1024,1664]{1,0:T(8,128)(2,1)} custom-call(s32[1]{0:T(128)} %bitcast.2.block_ref, bf16[512,1664]{1,0:T(8,128)(2,1)S(1)} %bitcast.18, f32[64,1,128]{2,1,0:T(1,128)S(1)} %copy.24.stored_ref), custom_call_target="tpu_custom_call" | custom-call | tf_op jit(solution)/shard_map/pallas_call | solution.py:133
  42.6 0.0 copy-start.1
  42.6 6.3 %all-to-all-start.1 = ((bf16[128,8,1664]{2,1,0:T(8,128)(2,1)}), bf16[128,8,1664]{2,1,0:T(8,128)(2,1)S(1)}, u32[]{:S(2)}, u32[]{:S(2)}) async-start(bf16[128,8,1664]{2,1,0:T(8,128)(2,1)} %bitcast.20), calls=%async_computation.1 | async-start | bytes 6815744 | tf_op jit(solution)/shard_map/all_to_all | solution.py:369
  48.8 1.1 collective-permute-start
  50.0 0.1 collective-permute-start.1
  50.1 0.4 collective-permute-start.2
  50.5 0.1 collective-permute-start.3
  50.6 0.4 collective-permute-start.4
  51.0 0.0 copy-done.1
  51.0 0.1 copy.22
  51.1 0.1 copy.21
  51.1 0.1 reshape.59
  51.2 0.1 dynamic_slice.7
  51.3 0.2 select_reduce_fusion.1
  51.5 0.1 compare_reduce_fusion
  52.3 5.2 %collective-permute-done.4 = bf16[512,256]{1,0:T(8,128)(2,1)} collective-permute-done((bf16[512,256]{1,0:T(8,128)(2,1)}, bf16[512,256]{1,0:T(8,128)(2,1)}, u32[]{:S(2)}, u32[]{:S(2)}) %collective-permute-start.4) | collective-permute-done | bytes 262176 | tf_op jit(solution)/shard_map/ppermute | solution.py:354
  57.5 1.9 %broadcast_select_fusion = (bf16[512,256]{1,0:T(8,128)(2,1)}, bf16[512,256]{1,0:T(8,128)(2,1)}) fusion(bf16[512,256]{1,0:T(8,128)(2,1)} %collective-permute-done.4, bf16[512,256]{1,0:T(8,128)(2,1)} %param.21, pred[]{:T(512)S(6)} %eq.61), kind=kLoop, calls=%fused_computation.3 | loop fusion | flops 262144 | bytes 1048577 | tf_op jit(solution)/shard_map/jit(_where)/select_n | solution.py:360
  59.3 0.0 collective-permute-done.refs_3_
  59.3 0.0 collective-permute-done.1.refs_4_
  59.3 0.0 collective-permute-done.2.refs_5_
  59.3 0.0 collective-permute-done.3.refs_7_
  59.4 34.1 %all-to-all-done.1 = bf16[128,8,1664]{2,1,0:T(8,128)(2,1)S(1)} async-done(((bf16[128,8,1664]{2,1,0:T(8,128)(2,1)}), bf16[128,8,1664]{2,1,0:T(8,128)(2,1)S(1)}, u32[]{:S(2)}, u32[]{:S(2)}) %all-to-all-start.1) | async-done | bytes 3407904 | tf_op jit(solution)/shard_map/all_to_all | solution.py:369
  93.5 28.3 %shard_map.133 = bf16[64,2,8,128]{3,2,1,0:T(8,128)(2,1)} custom-call(s32[8]{0:T(128)S(1)} %compare_select_fusion.owner_ref, bf16[16,4,2,8,1664]{4,3,2,1,0:T(8,128)(2,1)S(1)} %bitcast.17, bf16[1024,512]{1,0:T(8,128)(2,1)} %refs_0_.1, bf16[1024,512]{1,0:T(8,128)(2,1)} %refs_1_.1, bf16[1024,512]{1,0:T(8,128)(2,1)} %refs_2_.1, ...), custom_call_target="tpu_custom_call" | custom-call | tf_op jit(solution)/shard_map/pallas_call | solution.py:292
  121.8 4.3 %all-to-all-start.2 = ((bf16[128,8,128]{2,1,0:T(8,128)(2,1)}), bf16[128,8,128]{2,1,0:T(8,128)(2,1)S(1)}, u32[]{:S(2)}, u32[]{:S(2)}) async-start(bf16[128,8,128]{2,1,0:T(8,128)(2,1)} %bitcast.23), calls=%async_computation.2 | async-start | bytes 524288 | tf_op jit(solution)/shard_map/all_to_all | solution.py:387
  126.1 0.4 and_convert_fusion
  126.4 2.1 %broadcast_in_dim.35 = bf16[8,8,64,2,8]{4,3,2,1,0:T(2,128)(2,1)S(1)} broadcast(bf16[8,8,64,8]{3,2,1,0:T(8,128)(2,1)S(1)} %and_convert_fusion), dimensions={0,1,2,4} | broadcast | bytes 196608 | tf_op jit(solution)/shard_map/broadcast_in_dim | solution.py:393
  128.5 3.0 %reshape.58.place_ref = bf16[64,1024]{1,0:T(8,128)(2,1)S(1)} reshape(bf16[8,8,64,2,8]{4,3,2,1,0:T(2,128)(2,1)S(1)} %broadcast_in_dim.35) | data formatting | bytes 262144 | tf_op jit(solution)/shard_map/reshape | solution.py:393
  131.5 5.8 %all-to-all-done.2 = bf16[128,8,128]{2,1,0:T(8,128)(2,1)S(1)} async-done(((bf16[128,8,128]{2,1,0:T(8,128)(2,1)}), bf16[128,8,128]{2,1,0:T(8,128)(2,1)S(1)}, u32[]{:S(2)}, u32[]{:S(2)}) %all-to-all-start.2) | async-done | bytes 262176 | tf_op jit(solution)/shard_map/all_to_all | solution.py:387
  137.3 0.8 shard_map.134
  (7 shorter events, 0.0 us)
Async XLA Ops:
  3.0 12.0 %copy-start = (s32[64,16]{0,1:T(8,128)S(1)}, s32[64,16]{0,1:T(8,128)}, u32[]{:S(2)}) copy-start(s32[64,16]{0,1:T(8,128)} %param.14) | copy-start | bytes 12292
  3.0 12.1 %copy-start.2 = (s32[512]{0:T(512)S(1)}, s32[512]{0:T(512)}, u32[]{:S(2)}) copy-start(s32[512]{0:T(512)} %param.13) | copy-start | bytes 6148
  3.0 36.4 %all-to-all-start = ((bf16[64,8,1664]{2,1,0:T(8,128)(2,1)}), bf16[64,8,1664]{2,1,0:T(8,128)(2,1)S(1)}, u32[]{:S(2)}, u32[]{:S(2)}) async-start(bf16[64,8,1664]{2,1,0:T(8,128)(2,1)} %bitcast.21), calls=%async_computation | async-start | bytes 3407872 | tf_op jit(solution)/shard_map/all_to_all | solution.py:352
  42.6 8.5 %copy-start.1 = (s32[1,8,2]{1,2,0:T(2,128)S(1)}, s32[1,8,2]{1,2,0:T(2,128)}, u32[]{:S(2)}) copy-start(s32[1,8,2]{1,2,0:T(2,128)} %param.15) | copy-start | bytes 196
  42.6 50.9 %all-to-all-start.1 = ((bf16[128,8,1664]{2,1,0:T(8,128)(2,1)}), bf16[128,8,1664]{2,1,0:T(8,128)(2,1)S(1)}, u32[]{:S(2)}, u32[]{:S(2)}) async-start(bf16[128,8,1664]{2,1,0:T(8,128)(2,1)} %bitcast.20), calls=%async_computation.1 | async-start | bytes 6815744 | tf_op jit(solution)/shard_map/all_to_all | solution.py:369
  48.8 10.5 %collective-permute-start = (bf16[1024,512]{1,0:T(8,128)(2,1)}, bf16[1024,512]{1,0:T(8,128)(2,1)}, u32[]{:S(2)}, u32[]{:S(2)}) collective-permute-start(bf16[1024,512]{1,0:T(8,128)(2,1)} %refs_0_.1), channel_id=1, source_target_pairs={{0,1},{1,0},{2,3},{3,2},{4,5},{5,4},{6,7},{7,6},{8,9},{9,8},{10,11... | collective-permute-start | bytes 3145736 | tf_op jit(solution)/shard_map/ppermute | solution.py:354
  50.0 9.4 %collective-permute-start.1 = (bf16[1024,512]{1,0:T(8,128)(2,1)}, bf16[1024,512]{1,0:T(8,128)(2,1)}, u32[]{:S(2)}, u32[]{:S(2)}) collective-permute-start(bf16[1024,512]{1,0:T(8,128)(2,1)} %refs_1_.1), channel_id=1, source_target_pairs={{0,1},{1,0},{2,3},{3,2},{4,5},{5,4},{6,7},{7,6},{8,9},{9,8},{10,11... | collective-permute-start | bytes 3145736 | tf_op jit(solution)/shard_map/ppermute | solution.py:354
  50.1 9.3 %collective-permute-start.2 = (bf16[1024,512]{1,0:T(8,128)(2,1)}, bf16[1024,512]{1,0:T(8,128)(2,1)}, u32[]{:S(2)}, u32[]{:S(2)}) collective-permute-start(bf16[1024,512]{1,0:T(8,128)(2,1)} %refs_2_.1), channel_id=1, source_target_pairs={{0,1},{1,0},{2,3},{3,2},{4,5},{5,4},{6,7},{7,6},{8,9},{9,8},{10,11... | collective-permute-start | bytes 3145736 | tf_op jit(solution)/shard_map/ppermute | solution.py:354
  50.5 8.9 %collective-permute-start.3 = (bf16[512,1024]{1,0:T(8,128)(2,1)}, bf16[512,1024]{1,0:T(8,128)(2,1)}, u32[]{:S(2)}, u32[]{:S(2)}) collective-permute-start(bf16[512,1024]{1,0:T(8,128)(2,1)} %refs_6_.1), channel_id=1, source_target_pairs={{0,1},{1,0},{2,3},{3,2},{4,5},{5,4},{6,7},{7,6},{8,9},{9,8},{10,11... | collective-permute-start | bytes 3145736 | tf_op jit(solution)/shard_map/ppermute | solution.py:354
  50.6 6.9 %collective-permute-start.4 = (bf16[512,256]{1,0:T(8,128)(2,1)}, bf16[512,256]{1,0:T(8,128)(2,1)}, u32[]{:S(2)}, u32[]{:S(2)}) collective-permute-start(bf16[512,256]{1,0:T(8,128)(2,1)} %param.21), channel_id=1, source_target_pairs={{0,1},{1,0},{2,3},{3,2},{4,5},{5,4},{6,7},{7,6},{8,9},{9,8},{10,11... | collective-permute-start | bytes 786440 | tf_op jit(solution)/shard_map/ppermute | solution.py:354
  121.8 15.5 %all-to-all-start.2 = ((bf16[128,8,128]{2,1,0:T(8,128)(2,1)}), bf16[128,8,128]{2,1,0:T(8,128)(2,1)S(1)}, u32[]{:S(2)}, u32[]{:S(2)}) async-start(bf16[128,8,128]{2,1,0:T(8,128)(2,1)} %bitcast.23), calls=%async_computation.2 | async-start | bytes 524288 | tf_op jit(solution)/shard_map/all_to_all | solution.py:387
